TPU v7x, 32 devices: a whole 2x2x4 slice. The times are simulated.
32 devices in a mesh: probe: 4 (over y, core), ex: 8 (over z, x).
Axes of the slice: x: 2, y: 2, z: 4, core: 2. Of those that a mesh axis runs over, the one named last changes fastest.
Arguments:
- tokens: bfloat16 [2048, 768], P('ex'), may hold values from -6 to 6
- segment_ids: int32 [2048], replicated, may hold values from 0 to 6, as said below
- qkv_weight: bfloat16 [768, 2304], replicated, may hold values from -0.21875 to 0.21875
- qkv_bias: bfloat16 [2304], replicated, may hold values from -4 to 4
- out_weight: bfloat16 [768, 768], replicated, may hold values from -1.75 to 1.75
- out_bias: bfloat16 [768], replicated, may hold values from -6 to 6
- up_weight: bfloat16 [768, 3072], replicated, may hold values from -0.21875 to 0.21875
- up_bias: bfloat16 [3072], replicated, may hold values from -4 to 4
- down_weight: bfloat16 [3072, 768], replicated, may hold values from -0.109375 to 0.109375
- down_bias: bfloat16 [768], replicated, may hold values from -6 to 6
- norm1_gain: float32 [768], replicated, may hold values from 0.1 to 1.9
- norm1_bias: float32 [768], replicated, may hold values from -4 to 4
- norm2_gain: float32 [768], replicated, may hold values from 0.1 to 1.9
- norm2_bias: float32 [768], replicated, may hold values from -4 to 4
- probe_dirs: bfloat16 [16, 768, 3072], P('probe', 'ex'), may hold values from -0.21875 to 0.21875
- out_grad: bfloat16 [2048, 768], P('ex'), may hold values from -6 to 6
Outputs:
- layer_out: bfloat16 [2048, 768], P('ex')
- input_grad: bfloat16 [2048, 768], P('ex')
- grad_qkv_weight: float32 [768, 2304], P('ex')
- grad_qkv_bias: float32 [2304], replicated
- grad_out_weight: float32 [768, 768], P('ex')
- grad_out_bias: float32 [768], replicated
- grad_up_weight: float32 [768, 3072], P('ex')
- grad_up_bias: float32 [3072], replicated
- grad_down_weight: float32 [3072, 768], P('ex')
- grad_down_bias: float32 [768], replicated
- grad_norm1_gain: float32 [768], replicated
- grad_norm1_bias: float32 [768], replicated
- grad_norm2_gain: float32 [768], replicated
- grad_norm2_bias: float32 [768], replicated
- curvature: float32 [16, 768, 3072], P('probe', 'ex')
- probe_scores: float32 [16, 1], P('probe')
Inputs may be any that keep to these rules, and one draw needn't show every extreme that they name: `segment_ids`: along each row of 2048 tokens the ids never fall; no id occurs in two rows.
All inputs are finite; a program needn't handle non-finite values.
Results may differ from a plain program's by a relative error of at most 0.012.
Values may be sent and summed in bfloat16 or wider, within the bound.
No kernel may reach another device: no remote copies, remote signals or barrier semaphores. Data moves between devices by JAX's collectives and lax.ppermute only.
A program may use at most 256 MiB of HBM per device.

v0:
```python
import jax
import jax.numpy as jnp
from jax import lax
from jax.sharding import PartitionSpec as P

HEADS = 12
HEAD_DIM = 64
ROT = 16
SEQ = 2048


highest = lax.Precision.HIGHEST
eps_norm = 1e-05
masked_score = -1e30


def passed_along(block, axis, distance):
    devices = range(lax.axis_size(axis))
    route = [(i - distance, i) for i in devices if i - distance in devices]
    return lax.ppermute(block, axis, route)


def layer_norm(features, gain_vec, shift_vec):
    center = jnp.mean(features, axis=-1, keepdims=True)
    centred = features - center
    spread = jnp.mean(centred * centred, axis=-1, keepdims=True)
    return centred * lax.rsqrt(spread + eps_norm) * gain_vec + shift_vec


def gelu_exact(features):
    return jax.nn.gelu(features, approximate=False)


def rotary_tables(positions):
    steps = jnp.arange(ROT // 2, dtype=jnp.float32) * (2.0 / ROT)
    inverse = jnp.power(10000.0, -steps)
    angles = positions.astype(jnp.float32)[:, None] * inverse[None, :]
    angles = jnp.concatenate([angles, angles], axis=1)
    return (jnp.cos(angles), jnp.sin(angles))


def rotate(features, cosine, sine_part):
    turned = features[..., :ROT]
    rest_dims = features[..., ROT:]
    first_half = turned[..., : ROT // 2]
    second_half = turned[..., ROT // 2 :]
    half_turn = jnp.concatenate([-second_half, first_half], axis=-1)
    turned = turned * cosine[:, None, :] + half_turn * sine_part[:, None, :]
    return jnp.concatenate([turned, rest_dims], axis=-1)


def on_device(
    tokens,
    segment_ids,
    qkv_weight,
    qkv_bias,
    out_weight,
    out_bias,
    up_weight,
    up_bias,
    down_weight,
    down_bias,
    norm1_gain,
    norm1_bias,
    norm2_gain,
    norm2_bias,
    probe_dirs,
    out_grad,
):
    tok_count = tokens.shape[0]
    feature_width = tokens.shape[1]
    hidden_width = up_weight.shape[1]
    probe_count = probe_dirs.shape[0]
    groups = lax.axis_size("ex")
    ex_place = lax.axis_index("ex")
    blocks_per_row = SEQ // tok_count
    tok_start = ex_place * tok_count
    token_place = jnp.arange(tok_count)
    query_place = jnp.arange(tok_count)
    positions = (tok_start + query_place) % SEQ
    cosine, sine_part = rotary_tables(positions)
    score_scale = HEAD_DIM ** (-0.5)
    query_shape = (tok_count, HEADS, HEAD_DIM)
    head_shape = (tok_count, HEADS, HEAD_DIM)
    inputs = tokens.astype(jnp.float32)
    cotangent = out_grad.astype(jnp.float32)
    own_segments = lax.dynamic_slice_in_dim(segment_ids, tok_start, tok_count)
    query_segments = lax.dynamic_slice_in_dim(segment_ids, tok_start, tok_count)

    def turn(features):
        return rotate(features, cosine, sine_part)

    normed_one, norm_back_one = jax.vjp(layer_norm, inputs, norm1_gain, norm1_bias)
    normed_one_low = normed_one.astype(jnp.bfloat16)
    mixed_proj = jnp.dot(normed_one_low, qkv_weight, preferred_element_type=jnp.float32) + qkv_bias
    mixed_proj = mixed_proj.reshape(tok_count, HEADS, 3 * HEAD_DIM)
    raw_queries = mixed_proj[..., :HEAD_DIM]
    queries = turn(raw_queries).astype(jnp.bfloat16)
    key_rows = turn(mixed_proj[..., HEAD_DIM : 2 * HEAD_DIM]).astype(jnp.bfloat16)
    value_rows = mixed_proj[..., 2 * HEAD_DIM :].astype(jnp.bfloat16)
    local_pack = jnp.stack(
        [key_rows.reshape(tok_count, feature_width), value_rows.reshape(tok_count, feature_width)]
    )
    block_index = ex_place % blocks_per_row
    causal = token_place[None, :] <= query_place[:, None]
    block_list = [(local_pack, (query_segments[:, None] == own_segments[None, :]) & causal)]
    for distance in range(1, blocks_per_row):
        moved_pack = passed_along(local_pack, "ex", distance)
        source_start = jnp.maximum(tok_start - distance * tok_count, 0)
        block_segments = lax.dynamic_slice_in_dim(segment_ids, source_start, tok_count)
        same_doc = (query_segments[:, None] == block_segments[None, :]) & (block_index >= distance)
        block_list.append((moved_pack, same_doc))

    def block_scores(kv_pack, allowed):
        block_keys = kv_pack[0].reshape(head_shape)
        raw_scores = (
            jnp.einsum("qhd,khd->hqk", queries, block_keys, preferred_element_type=jnp.float32)
            * score_scale
        )
        return jnp.where(allowed[None], raw_scores, masked_score)

    score_list = [block_scores(kv_pack, allowed) for kv_pack, allowed in block_list]
    row_top = jnp.max(score_list[0], axis=-1, keepdims=True)
    for scores_now in score_list[1:]:
        row_top = jnp.maximum(row_top, jnp.max(scores_now, axis=-1, keepdims=True))
    row_total = jnp.zeros_like(row_top)
    for scores_now in score_list:
        row_total = row_total + jnp.sum(jnp.exp(scores_now - row_top), axis=-1, keepdims=True)
    log_total = row_top + jnp.log(row_total)
    attended = jnp.zeros(query_shape, jnp.float32)
    for distance in range(blocks_per_row):
        prob_low = jnp.exp(score_list[distance] - log_total).astype(jnp.bfloat16)
        block_values = block_list[distance][0][1].reshape(head_shape)
        attended = attended + jnp.einsum(
            "hqk,khd->qhd", prob_low, block_values, preferred_element_type=jnp.float32
        )
    attended_low = attended.reshape(tok_count, feature_width).astype(jnp.bfloat16)
    attn_branch = jnp.dot(attended_low, out_weight, preferred_element_type=jnp.float32) + out_bias
    normed_two, norm_back_two = jax.vjp(layer_norm, inputs, norm2_gain, norm2_bias)
    normed_two_low = normed_two.astype(jnp.bfloat16)
    hidden = jnp.dot(normed_two_low, up_weight, preferred_element_type=jnp.float32) + up_bias
    active, gelu_back = jax.vjp(gelu_exact, hidden)
    active_low = active.astype(jnp.bfloat16)
    mlp_branch = jnp.dot(active_low, down_weight, preferred_element_type=jnp.float32) + down_bias
    layer_out = (inputs + attn_branch + mlp_branch).astype(jnp.bfloat16)
    grad_down_weight = jnp.einsum(
        "tf,td->fd", active_low, out_grad, preferred_element_type=jnp.float32
    )
    grad_out_weight = jnp.einsum(
        "te,td->ed", attended_low, out_grad, preferred_element_type=jnp.float32
    )
    grad_down_bias = jnp.sum(cotangent, axis=0)
    grad_out_bias = jnp.sum(cotangent, axis=0)
    upstream = jnp.einsum("td,fd->tf", out_grad, down_weight, preferred_element_type=jnp.float32)
    hidden_grad = gelu_back(upstream)[0].astype(jnp.bfloat16)
    grad_up_weight = jnp.einsum(
        "td,tf->df", normed_two_low, hidden_grad, preferred_element_type=jnp.float32
    )
    grad_up_bias = jnp.sum(hidden_grad.astype(jnp.float32), axis=0)
    normed_two_grad = jnp.einsum(
        "tf,df->td", hidden_grad, up_weight, preferred_element_type=jnp.float32
    )
    attended_grad = (
        jnp.einsum("td,ed->te", out_grad, out_weight, preferred_element_type=jnp.float32)
        .astype(jnp.bfloat16)
        .reshape(query_shape)
    )

    def block_probs(kv_pack, allowed):
        prob_rows = jnp.exp(block_scores(kv_pack, allowed) - log_total)
        prob_grad = jnp.einsum(
            "qhd,khd->hqk",
            attended_grad,
            kv_pack[1].reshape(head_shape),
            preferred_element_type=jnp.float32,
        )
        return (prob_rows, prob_grad)

    delta_rows = jnp.zeros_like(log_total)
    for kv_pack, allowed in block_list:
        prob_rows, prob_grad = block_probs(kv_pack, allowed)
        delta_rows = delta_rows + jnp.sum(prob_rows * prob_grad, axis=-1, keepdims=True)
    query_grad = jnp.zeros(query_shape, jnp.float32)
    kv_grad = jnp.zeros((2, tok_count, feature_width), jnp.float32)
    for distance in range(blocks_per_row):
        kv_pack, allowed = block_list[distance]
        prob_rows, prob_grad = block_probs(kv_pack, allowed)
        score_grad = (prob_rows * (prob_grad - delta_rows)).astype(jnp.bfloat16)
        block_keys = kv_pack[0].reshape(head_shape)
        query_grad = (
            query_grad
            + jnp.einsum("hqk,khd->qhd", score_grad, block_keys, preferred_element_type=jnp.float32)
            * score_scale
        )
        key_grad = (
            jnp.einsum("hqk,qhd->khd", score_grad, queries, preferred_element_type=jnp.float32)
            * score_scale
        )
        value_grad = jnp.einsum(
            "hqk,qhd->khd",
            prob_rows.astype(jnp.bfloat16),
            attended_grad,
            preferred_element_type=jnp.float32,
        )
        pack_grad = jnp.stack(
            [
                key_grad.reshape(tok_count, feature_width),
                value_grad.reshape(tok_count, feature_width),
            ]
        )
        if distance == 0:
            kv_grad = pack_grad
        else:
            kv_grad = kv_grad + passed_along(pack_grad, "ex", -distance)
    turn_back = jax.vjp(turn, raw_queries)[1]
    query_back = turn_back(query_grad)[0]
    key_back = turn_back(kv_grad[0].reshape(query_shape))[0]
    mixed_grad = jnp.concatenate([query_back, key_back, kv_grad[1].reshape(query_shape)], axis=-1)
    mixed_grad = mixed_grad.reshape(tok_count, 3 * feature_width).astype(jnp.bfloat16)
    grad_qkv_weight = jnp.einsum(
        "td,te->de", normed_one_low, mixed_grad, preferred_element_type=jnp.float32
    )
    grad_qkv_bias = jnp.sum(mixed_grad.astype(jnp.float32), axis=0)
    normed_one_grad = jnp.einsum(
        "te,de->td", mixed_grad, qkv_weight, preferred_element_type=jnp.float32
    )
    input_term_one, grad_norm1_gain, grad_norm1_bias = norm_back_one(normed_one_grad)
    input_term_two, grad_norm2_gain, grad_norm2_bias = norm_back_two(normed_two_grad)
    input_grad = (cotangent + input_term_one + input_term_two).astype(jnp.bfloat16)

    def slope(pre_act):
        return jax.vjp(gelu_exact, pre_act)[1](upstream)[0]

    curve_factor = jax.vjp(slope, hidden)[1](jnp.ones_like(hidden))[0]
    columns = normed_two_low
    probe_along = jnp.einsum(
        "tc,pcf->tpf",
        columns,
        lax.all_gather(probe_dirs, "ex", axis=1, tiled=True),
        preferred_element_type=jnp.float32,
    )
    weighted = (
        (probe_along * curve_factor[:, None, :])
        .astype(jnp.bfloat16)
        .reshape(tok_count, probe_count * hidden_width)
    )
    local_rows = feature_width // groups
    columns = normed_two_low
    curvature = lax.psum_scatter(
        jnp.einsum("tc,tq->cq", columns, weighted, preferred_element_type=jnp.float32),
        "ex",
        scatter_dimension=0,
        tiled=True,
    )
    curvature = curvature.reshape(local_rows, probe_count, hidden_width).transpose(1, 0, 2)
    token_scores = jnp.einsum(
        "tpf,tf->p", probe_along, hidden_grad.astype(jnp.float32), precision=highest
    )
    total_rows = groups * tok_count // SEQ
    row_pick = (jnp.arange(total_rows) == tok_start // SEQ).astype(jnp.float32)
    score_term = token_scores[:, None] * row_pick[None, :]
    small_list = [
        grad_qkv_bias,
        grad_out_bias,
        grad_up_bias,
        grad_down_bias,
        grad_norm1_gain,
        grad_norm1_bias,
        grad_norm2_gain,
        grad_norm2_bias,
    ]
    small_flat = jnp.concatenate(small_list)
    probe_scores, small_total = lax.psum((score_term, small_flat), "ex")
    qkv_part, out_part, up_part, down_part = (
        lax.psum_scatter(grad_qkv_weight, "ex", scatter_dimension=0, tiled=True),
        lax.psum_scatter(grad_out_weight, "ex", scatter_dimension=0, tiled=True),
        lax.psum_scatter(grad_up_weight, "ex", scatter_dimension=0, tiled=True),
        lax.psum_scatter(grad_down_weight, "ex", scatter_dimension=0, tiled=True),
    )
    small_results = []
    offset_now = 0
    for member in small_list:
        length = member.shape[0]
        small_results.append(small_total[offset_now : offset_now + length])
        offset_now = offset_now + length
    return (
        layer_out,
        input_grad,
        qkv_part,
        small_results[0],
        out_part,
        small_results[1],
        up_part,
        small_results[2],
        down_part,
        small_results[3],
        small_results[4],
        small_results[5],
        small_results[6],
        small_results[7],
        curvature,
        probe_scores,
    )


def solution(mesh):
    in_specs = (
        P("ex", None),
        P(),
        P(),
        P(),
        P(),
        P(),
        P(),
        P(),
        P(),
        P(),
        P(),
        P(),
        P(),
        P(),
        P("probe", "ex", None),
        P("ex", None),
    )
    out_specs = (
        P("ex", None),
        P("ex", None),
        P("ex", None),
        P(),
        P("ex", None),
        P(),
        P("ex", None),
        P(),
        P("ex", None),
        P(),
        P(),
        P(),
        P(),
        P(),
        P("probe", "ex", None),
        P("probe", None),
    )
    return jax.shard_map(
        on_device, mesh=mesh, in_specs=in_specs, out_specs=out_specs, check_vma=False
    )
```

profile of v0, /device:TPU:1, one launch (start us, length us, event | category | flops | bytes accessed | tf_op | source)
XLA Modules:
  0.0 1958.6 jit_solution(9487418646126565092)
XLA Ops:
  12.1 4.0 convolution_add_fusion.1
  17.8 11.4 bitcast_convert_fusion
  29.2 345.0 %all-gather.2.cloned.1.call-done = bf16[4,768,3072]{2,1,0:T(8,128)(2,1)} async-done(((bf16[4,96,3072]{2,1,0:T(8,128)(2,1)}), bf16[4,768,3072]{2,1,0:T(8,128)(2,1)}) %all-gather.2.cloned.1.call-update) | async-done | bytes 18874384 | tf_op jit(solution)/shard_map/all_gather | solution.py:239
  374.2 13.2 multiply_reduce_fusion
  387.4 10.2 multiply_convert_fusion
  397.5 8.6 copy.123
  406.1 16.9 fusion.147
  424.1 3.6 convolution_add_fusion
  427.6 3.1 copy.89
  442.2 6.0 collective-permute-start.6
  456.9 2.7 convolution_convert_fusion
  461.5 3.4 fusion.139
  471.8 9.9 collective-permute-done.6
  484.9 30.4 %collective-permute-done.5 = bf16[2,256,768]{1,2,0:T(8,128)(2,1)} collective-permute-done((bf16[2,256,768]{1,2,0:T(8,128)(2,1)}, bf16[2,256,768]{1,2,0:T(8,128)(2,1)}, u32[]{:S(2)}, u32[]{:S(2)}) %collective-permute-start.5) | collective-permute-done | bytes 786464 | tf_op jit(solution)/shard_map/ppermute | solution.py:20
  518.6 29.2 %collective-permute-done.4 = bf16[2,256,768]{1,2,0:T(8,128)(2,1)} collective-permute-done((bf16[2,256,768]{1,2,0:T(8,128)(2,1)}, bf16[2,256,768]{1,2,0:T(8,128)(2,1)}, u32[]{:S(2)}, u32[]{:S(2)}) %collective-permute-start.4) | collective-permute-done | bytes 786464 | tf_op jit(solution)/shard_map/ppermute | solution.py:20
  549.8 24.0 %collective-permute-done.3 = bf16[2,256,768]{1,2,0:T(8,128)(2,1)} collective-permute-done((bf16[2,256,768]{1,2,0:T(8,128)(2,1)}, bf16[2,256,768]{1,2,0:T(8,128)(2,1)}, u32[]{:S(2)}, u32[]{:S(2)}) %collective-permute-start.3) | collective-permute-done | bytes 786464 | tf_op jit(solution)/shard_map/ppermute | solution.py:20
  575.7 18.3 collective-permute-done.2
  595.9 31.8 %collective-permute-done.1 = bf16[2,256,768]{1,2,0:T(8,128)(2,1)S(1)} collective-permute-done((bf16[2,256,768]{1,2,0:T(8,128)(2,1)}, bf16[2,256,768]{1,2,0:T(8,128)(2,1)S(1)}, u32[]{:S(2)}, u32[]{:S(2)}) %collective-permute-start.1) | collective-permute-done | bytes 786464 | tf_op jit(solution)/shard_map/ppermute | solution.py:20
  627.8 2.3 fusion.14
  635.6 10.0 exponential_reduce_fusion.6
  646.4 3.4 fusion.177
  650.4 2.6 fusion.174
  655.3 2.3 fusion.176
  658.1 4.0 multiply_reduce_fusion.2
  662.1 13.0 multiply_reduce_fusion.7
  676.0 8.5 multiply_convert_fusion.3
  696.8 13.0 multiply_convert_fusion.8
  711.9 2.8 fusion.89
  740.4 3.8 fusion.97
  752.6 3.6 collective-permute-done.13
  757.5 7.3 collective-permute-done.12
  771.7 195.9 %collective-permute-done.11 = f32[2,256,768]{1,2,0:T(8,128)} collective-permute-done((f32[2,256,768]{1,2,0:T(8,128)}, f32[2,256,768]{1,2,0:T(8,128)}, u32[]{:S(2)}, u32[]{:S(2)}) %collective-permute-start.11) | collective-permute-done | bytes 1572896 | tf_op jit(solution)/shard_map/ppermute | solution.py:20
  967.6 32.7 %collective-permute-done.10 = f32[2,256,768]{1,2,0:T(8,128)} collective-permute-done((f32[2,256,768]{1,2,0:T(8,128)}, f32[2,256,768]{1,2,0:T(8,128)}, u32[]{:S(2)}, u32[]{:S(2)}) %collective-permute-start.10) | collective-permute-done | bytes 1572896 | tf_op jit(solution)/shard_map/ppermute | solution.py:20
  1000.3 4.1 fusion.28
  1007.6 4.2 fusion.142
  1012.5 6.7 fusion.150
  1019.5 3.4 multiply_convert_fusion.9
  1024.1 5.1 fusion.186
  1033.4 5.3 fusion.184
  1038.8 3.9 convolution_add_fusion.7
  1046.7 3.1 fusion.162
  1059.7 154.4 %all-reduce.8 = (f32[9984]{0:T(1024)}, f32[4,1]{0,1:T(1,128)}) all-reduce(f32[9984]{0:T(1024)} %constant_dynamic-update-slice_fusion, f32[4,1]{0,1:T(1,128)S(1)} %multiply_bitcast_fusion), channel_id=1, replica_groups=mesh['probe'=4,'ex'=8] {'ex'}, use_global_device_ids=true, to_apply=%region_38.39 | all-reduce | flops 9988 | bytes 79904 | tf_op jit(solution)/shard_map/psum | solution.py:273
  1218.1 194.6 %reduce-scatter.14.cloned.1.call-done = f32[96,12288]{1,0:T(8,128)} async-done(((f32[768,12288]{1,0:T(8,128)}), f32[96,12288]{1,0:T(8,128)}) %reduce-scatter.14.cloned.1.call-update) | async-done | bytes 4718608 | tf_op jit(solution)/shard_map/reduce_scatter | solution.py:249
  1412.7 5.1 copy.166
  1417.7 66.6 %reduce-scatter.8.cloned.1.call-done = f32[96,768]{1,0:T(8,128)} async-done(((f32[768,768]{1,0:T(8,128)}), f32[96,768]{1,0:T(8,128)}) %reduce-scatter.8.cloned.1.call-update) | async-done | bytes 294928 | tf_op jit(solution)/shard_map/reduce_scatter | solution.py:276
  1484.4 132.7 %reduce-scatter.6.cloned.1.call-done = f32[96,2304]{1,0:T(8,128)} async-done(((f32[768,2304]{1,0:T(8,128)}), f32[96,2304]{1,0:T(8,128)}) %reduce-scatter.6.cloned.1.call-update) | async-done | bytes 884752 | tf_op jit(solution)/shard_map/reduce_scatter | solution.py:275
  1617.1 167.5 %reduce-scatter.10.cloned.1.call-done = f32[96,3072]{1,0:T(8,128)} async-done(((f32[768,3072]{1,0:T(8,128)}), f32[96,3072]{1,0:T(8,128)}) %reduce-scatter.10.cloned.1.call-update) | async-done | bytes 1179664 | tf_op jit(solution)/shard_map/reduce_scatter | solution.py:277
  1784.6 166.6 %reduce-scatter.12.cloned.1.call-done = f32[384,768]{1,0:T(8,128)} async-done(((f32[3072,768]{1,0:T(8,128)}), f32[384,768]{1,0:T(8,128)}) %reduce-scatter.12.cloned.1.call-update) | async-done | bytes 1179664 | tf_op jit(solution)/shard_map/reduce_scatter | solution.py:278
  (415 shorter events, 142.4 us)
Async XLA Ops:
  7.2 416.9 %copy-start = (bf16[768,2304]{1,0:T(8,128)(2,1)S(1)}, bf16[768,2304]{1,0:T(8,128)(2,1)}, u32[]{:S(2)}) copy-start(bf16[768,2304]{1,0:T(8,128)(2,1)} %param.18) | copy-start | bytes 10616836
  7.2 366.9 %all-gather.2.cloned.1.call-start = ((), (), s32[]{:S(2)}) async-start(), calls=%async_computation.9 | async-start | bytes 21233664 | tf_op jit(solution)/shard_map/all_gather | solution.py:239
  8.0 1404.7 %reduce-scatter.14.cloned.1.call-start = ((), (), s32[]{:S(2)}) async-start(), calls=%async_computation.10 | async-start | bytes 42467328 | tf_op jit(solution)/shard_map/reduce_scatter | solution.py:249
  10.0 414.0 %copy-start.119 = (f32[256]{0:T(256)}, f32[256]{0:T(256)S(1)}, u32[]{:S(2)}) copy-start(f32[256]{0:T(256)S(1)} %broadcast_multiply_fusion.1) | copy-start | bytes 3076
  12.0 412.0 %copy-start.121 = (f32[256]{0:T(256)}, f32[256]{0:T(256)S(1)}, u32[]{:S(2)}) copy-start(f32[256]{0:T(256)S(1)} %fusion.76) | copy-start | bytes 3076
  423.1 1061.3 %reduce-scatter.8.cloned.1.call-start = ((), (), s32[]{:S(2)}) async-start(), calls=%async_computation.6 | async-start | bytes 2654208 | tf_op jit(solution)/shard_map/reduce_scatter | solution.py:276
  435.9 32.8 %copy-start.115 = (f32[256,16]{0,1:T(8,128)}, f32[256,16]{0,1:T(8,128)S(1)}, u32[]{:S(2)}) copy-start(f32[256,16]{0,1:T(8,128)S(1)} %get-tuple-element.104) | copy-start | bytes 49156
  442.2 39.4 %collective-permute-start.6 = (bf16[2,256,768]{1,2,0:T(8,128)(2,1)}, bf16[2,256,768]{1,2,0:T(8,128)(2,1)}, u32[]{:S(2)}, u32[]{:S(2)}) collective-permute-start(bf16[2,256,768]{1,2,0:T(8,128)(2,1)} %pad_maximum_fusion.7), channel_id=1, source_target_pairs={{0,7},{8,15},{16,23},{24,31}} | collective-permute-start | bytes 2359304 | tf_op jit(solution)/shard_map/ppermute | solution.py:20
  448.2 67.2 %collective-permute-start.5 = (bf16[2,256,768]{1,2,0:T(8,128)(2,1)}, bf16[2,256,768]{1,2,0:T(8,128)(2,1)}, u32[]{:S(2)}, u32[]{:S(2)}) collective-permute-start(bf16[2,256,768]{1,2,0:T(8,128)(2,1)} %pad_maximum_fusion.7), channel_id=1, source_target_pairs={{0,6},{1,7},{8,14},{9,15},{16,22},{17,23},{24,30},{25,31}} | collective-permute-start | bytes 2359304 | tf_op jit(solution)/shard_map/ppermute | solution.py:20
  450.4 97.5 %collective-permute-start.4 = (bf16[2,256,768]{1,2,0:T(8,128)(2,1)}, bf16[2,256,768]{1,2,0:T(8,128)(2,1)}, u32[]{:S(2)}, u32[]{:S(2)}) collective-permute-start(bf16[2,256,768]{1,2,0:T(8,128)(2,1)} %pad_maximum_fusion.7), channel_id=1, source_target_pairs={{0,5},{1,6},{2,7},{8,13},{9,14},{10,15},{16,21},{17,22},{18,23},{2... | collective-permute-start | bytes 2359304 | tf_op jit(solution)/shard_map/ppermute | solution.py:20
  452.5 121.2 %collective-permute-start.3 = (bf16[2,256,768]{1,2,0:T(8,128)(2,1)}, bf16[2,256,768]{1,2,0:T(8,128)(2,1)}, u32[]{:S(2)}, u32[]{:S(2)}) collective-permute-start(bf16[2,256,768]{1,2,0:T(8,128)(2,1)} %pad_maximum_fusion.7), channel_id=1, source_target_pairs={{0,4},{1,5},{2,6},{3,7},{8,12},{9,13},{10,14},{11,15},{16,20},{17,... | collective-permute-start | bytes 2359304 | tf_op jit(solution)/shard_map/ppermute | solution.py:20
  454.7 139.3 %collective-permute-start.2 = (bf16[2,256,768]{1,2,0:T(8,128)(2,1)}, bf16[2,256,768]{1,2,0:T(8,128)(2,1)}, u32[]{:S(2)}, u32[]{:S(2)}) collective-permute-start(bf16[2,256,768]{1,2,0:T(8,128)(2,1)} %pad_maximum_fusion.7), channel_id=1, source_target_pairs={{0,3},{1,4},{2,5},{3,6},{4,7},{8,11},{9,12},{10,13},{11,14},{12,15... | collective-permute-start | bytes 2359304 | tf_op jit(solution)/shard_map/ppermute | solution.py:20
  468.7 16.3 copy-start.91
  468.7 159.1 %copy-start.105 = (pred[256,256]{0,1:T(8,128)(4,1)}, pred[256,256]{0,1:T(8,128)(4,1)S(1)}, u32[]{:S(2)}) copy-start(pred[256,256]{0,1:T(8,128)(4,1)S(1)} %get-tuple-element.112) | copy-start | bytes 196612
  468.7 161.5 %copy-start.101 = (pred[256,256]{0,1:T(8,128)(4,1)}, pred[256,256]{0,1:T(8,128)(4,1)S(1)}, u32[]{:S(2)}) copy-start(pred[256,256]{0,1:T(8,128)(4,1)S(1)} %get-tuple-element.111) | copy-start | bytes 196612
  468.7 162.2 %copy-start.98 = (pred[256,256]{0,1:T(8,128)(4,1)}, pred[256,256]{0,1:T(8,128)(4,1)S(1)}, u32[]{:S(2)}) copy-start(pred[256,256]{0,1:T(8,128)(4,1)S(1)} %get-tuple-element.110) | copy-start | bytes 196612
  468.7 162.9 %copy-start.96 = (pred[256,256]{0,1:T(8,128)(4,1)}, pred[256,256]{0,1:T(8,128)(4,1)S(1)}, u32[]{:S(2)}) copy-start(pred[256,256]{0,1:T(8,128)(4,1)S(1)} %get-tuple-element.109) | copy-start | bytes 196612
  468.7 163.6 %copy-start.94 = (pred[256,256]{0,1:T(8,128)(4,1)}, pred[256,256]{0,1:T(8,128)(4,1)S(1)}, u32[]{:S(2)}) copy-start(pred[256,256]{0,1:T(8,128)(4,1)S(1)} %get-tuple-element.108) | copy-start | bytes 196612
  468.7 165.7 %copy-start.66 = (pred[256,256]{0,1:T(8,128)(4,1)}, pred[256,256]{0,1:T(8,128)(4,1)S(1)}, u32[]{:S(2)}) copy-start(pred[256,256]{0,1:T(8,128)(4,1)S(1)} %get-tuple-element.107) | copy-start | bytes 196612
  468.7 267.1 %copy-start.65 = (pred[256,256]{0,1:T(8,128)(4,1)}, pred[256,256]{0,1:T(8,128)(4,1)S(1)}, u32[]{:S(2)}) copy-start(pred[256,256]{0,1:T(8,128)(4,1)S(1)} %get-tuple-element.106) | copy-start | bytes 196612
  469.9 251.9 %copy-start.45 = (bf16[256,12,16]{0,2,1:T(8,128)(2,1)}, bf16[256,12,16]{0,2,1:T(8,128)(2,1)S(1)}, u32[]{:S(2)}) copy-start(bf16[256,12,16]{0,2,1:T(8,128)(2,1)S(1)} %fusion.71) | copy-start | bytes 294916
  471.8 162.7 %copy-start.10 = (f32[12,256,256]{1,2,0:T(8,128)}, f32[12,256,256]{1,2,0:T(8,128)S(1)}, u32[]{:S(2)}) copy-start(f32[12,256,256]{1,2,0:T(8,128)S(1)} %get-tuple-element.127) | copy-start | bytes 9437188
  481.7 146.0 %collective-permute-start.1 = (bf16[2,256,768]{1,2,0:T(8,128)(2,1)}, bf16[2,256,768]{1,2,0:T(8,128)(2,1)S(1)}, u32[]{:S(2)}, u32[]{:S(2)}) collective-permute-start(bf16[2,256,768]{1,2,0:T(8,128)(2,1)} %pad_maximum_fusion.7), channel_id=1, source_target_pairs={{0,2},{1,3},{2,4},{3,5},{4,6},{5,7},{8,10},{9,11},{10,12},{11,13},... | collective-permute-start | bytes 2359304 | tf_op jit(solution)/shard_map/ppermute | solution.py:20
  484.9 142.9 %copy-start.80 = (bf16[1,256,768]{1,2,0:T(8,128)(2,1)}, bf16[1,256,768]{1,2,0:T(8,128)(2,1)S(1)}, u32[]{:S(2)}) copy-start(bf16[1,256,768]{1,2,0:T(8,128)(2,1)S(1)} %get-tuple-element.68) | copy-start | bytes 1179652
  515.4 112.4 %collective-permute-start = (bf16[2,256,768]{1,2,0:T(8,128)(2,1)}, bf16[2,256,768]{1,2,0:T(8,128)(2,1)S(1)}, u32[]{:S(2)}, u32[]{:S(2)}) collective-permute-start(bf16[2,256,768]{1,2,0:T(8,128)(2,1)} %pad_maximum_fusion.7), channel_id=1, source_target_pairs={{0,1},{1,2},{2,3},{3,4},{4,5},{5,6},{6,7},{8,9},{9,10},{10,11},{11... | collective-permute-start | bytes 2359304 | tf_op jit(solution)/shard_map/ppermute | solution.py:20
  518.6 111.6 %copy-start.82 = (bf16[1,256,768]{1,2,0:T(8,128)(2,1)}, bf16[1,256,768]{1,2,0:T(8,128)(2,1)S(1)}, u32[]{:S(2)}) copy-start(bf16[1,256,768]{1,2,0:T(8,128)(2,1)S(1)} %get-tuple-element.67) | copy-start | bytes 1179652
  549.8 81.1 %copy-start.74 = (bf16[1,256,768]{1,2,0:T(8,128)(2,1)}, bf16[1,256,768]{1,2,0:T(8,128)(2,1)S(1)}, u32[]{:S(2)}) copy-start(bf16[1,256,768]{1,2,0:T(8,128)(2,1)S(1)} %get-tuple-element.65) | copy-start | bytes 1179652
  549.8 78.1 %copy-start.28 = (bf16[256,12,48]{0,2,1:T(8,128)(2,1)S(1)}, bf16[256,12,48]{0,2,1:T(8,128)(2,1)}, u32[]{:S(2)}) copy-start(bf16[256,12,48]{0,2,1:T(8,128)(2,1)} %slice.183) | copy-start | bytes 884740
  575.7 55.9 %copy-start.76 = (bf16[1,256,768]{1,2,0:T(8,128)(2,1)}, bf16[1,256,768]{1,2,0:T(8,128)(2,1)S(1)}, u32[]{:S(2)}) copy-start(bf16[1,256,768]{1,2,0:T(8,128)(2,1)S(1)} %get-tuple-element.63) | copy-start | bytes 1179652
  595.9 36.5 %copy-start.78 = (bf16[1,256,768]{1,2,0:T(8,128)(2,1)}, bf16[1,256,768]{1,2,0:T(8,128)(2,1)S(1)}, u32[]{:S(2)}) copy-start(bf16[1,256,768]{1,2,0:T(8,128)(2,1)S(1)} %get-tuple-element.61) | copy-start | bytes 1179652
  633.7 102.9 %copy-start.3 = (f32[12,256,256]{1,2,0:T(8,128)}, f32[12,256,256]{1,2,0:T(8,128)S(1)}, u32[]{:S(2)}) copy-start(f32[12,256,256]{1,2,0:T(8,128)S(1)} %get-tuple-element.125) | copy-start | bytes 9437188
  634.5 101.4 %copy-start.1 = (f32[12,256,256]{1,2,0:T(8,128)}, f32[12,256,256]{1,2,0:T(8,128)S(1)}, u32[]{:S(2)}) copy-start(f32[12,256,256]{1,2,0:T(8,128)S(1)} %get-tuple-element.129) | copy-start | bytes 9437188
  635.6 10.8 copy-start.7
  687.2 69.0 %collective-permute-start.13 = (f32[2,256,768]{1,2,0:T(8,128)}, f32[2,256,768]{1,2,0:T(8,128)}, u32[]{:S(2)}, u32[]{:S(2)}) collective-permute-start(f32[2,256,768]{1,2,0:T(8,128)} %pad_maximum_fusion.6), channel_id=1, source_target_pairs={{7,0},{15,8},{23,16},{31,24}} | collective-permute-start | bytes 4718600 | tf_op jit(solution)/shard_map/ppermute | solution.py:20
  691.4 73.4 %collective-permute-start.12 = (f32[2,256,768]{1,2,0:T(8,128)}, f32[2,256,768]{1,2,0:T(8,128)}, u32[]{:S(2)}, u32[]{:S(2)}) collective-permute-start(f32[2,256,768]{1,2,0:T(8,128)} %pad_maximum_fusion.5), channel_id=1, source_target_pairs={{6,0},{7,1},{14,8},{15,9},{22,16},{23,17},{30,24},{31,25}} | collective-permute-start | bytes 4718600 | tf_op jit(solution)/shard_map/ppermute | solution.py:20
  695.6 272.0 %collective-permute-start.11 = (f32[2,256,768]{1,2,0:T(8,128)}, f32[2,256,768]{1,2,0:T(8,128)}, u32[]{:S(2)}, u32[]{:S(2)}) collective-permute-start(f32[2,256,768]{1,2,0:T(8,128)} %pad_maximum_fusion.4), channel_id=1, source_target_pairs={{5,0},{6,1},{7,2},{13,8},{14,9},{15,10},{21,16},{22,17},{23,18},{2... | collective-permute-start | bytes 4718600 | tf_op jit(solution)/shard_map/ppermute | solution.py:20
  716.0 284.3 %collective-permute-start.10 = (f32[2,256,768]{1,2,0:T(8,128)}, f32[2,256,768]{1,2,0:T(8,128)}, u32[]{:S(2)}, u32[]{:S(2)}) collective-permute-start(f32[2,256,768]{1,2,0:T(8,128)} %pad_maximum_fusion.3), channel_id=1, source_target_pairs={{4,0},{5,1},{6,2},{7,3},{12,8},{13,9},{14,10},{15,11},{20,16},{21,... | collective-permute-start | bytes 4718600 | tf_op jit(solution)/shard_map/ppermute | solution.py:20
  720.2 280.1 %collective-permute-start.9 = (f32[2,256,768]{1,2,0:T(8,128)}, f32[2,256,768]{1,2,0:T(8,128)}, u32[]{:S(2)}, u32[]{:S(2)}) collective-permute-start(f32[2,256,768]{1,2,0:T(8,128)} %pad_maximum_fusion.2), channel_id=1, source_target_pairs={{3,0},{4,1},{5,2},{6,3},{7,4},{11,8},{12,9},{13,10},{14,11},{15,12... | collective-permute-start | bytes 4718600 | tf_op jit(solution)/shard_map/ppermute | solution.py:20
  745.7 871.4 %reduce-scatter.6.cloned.1.call-start = ((), (), s32[]{:S(2)}) async-start(), calls=%async_computation.5 | async-start | bytes 7962624 | tf_op jit(solution)/shard_map/reduce_scatter | solution.py:275
  751.6 14.7 copy-start.35
  751.6 14.7 copy-start.64
  751.6 14.7 copy-start.110
  752.2 14.6 copy-start.34
  752.2 14.6 copy-start.73
  756.2 244.1 %collective-permute-start.8 = (f32[2,256,768]{1,2,0:T(8,128)S(1)}, f32[2,256,768]{1,2,0:T(8,128)S(1)}, u32[]{:S(2)}, u32[]{:S(2)}) collective-permute-start(f32[2,256,768]{1,2,0:T(8,128)S(1)} %pad_maximum_fusion.1), channel_id=1, source_target_pairs={{2,0},{3,1},{4,2},{5,3},{6,4},{7,5},{10,8},{11,9},{12,10},{13,11},... | collective-permute-start | bytes 4718600 | tf_op jit(solution)/shard_map/ppermute | solution.py:20
  764.8 235.5 %collective-permute-start.7 = (f32[2,256,768]{1,2,0:T(8,128)S(1)}, f32[2,256,768]{1,2,0:T(8,128)S(1)}, u32[]{:S(2)}, u32[]{:S(2)}) collective-permute-start(f32[2,256,768]{1,2,0:T(8,128)S(1)} %pad_maximum_fusion), channel_id=1, source_target_pairs={{1,0},{2,1},{3,2},{4,3},{5,4},{6,5},{7,6},{9,8},{10,9},{11,10},{12... | collective-permute-start | bytes 4718600 | tf_op jit(solution)/shard_map/ppermute | solution.py:20
  1011.8 772.8 %reduce-scatter.10.cloned.1.call-start = ((), (), s32[]{:S(2)}) async-start(), calls=%async_computation.7 | async-start | bytes 10616832 | tf_op jit(solution)/shard_map/reduce_scatter | solution.py:277
  1019.2 932.1 %reduce-scatter.12.cloned.1.call-start = ((), (), s32[]{:S(2)}) async-start(), calls=%async_computation.8 | async-start | bytes 10616832 | tf_op jit(solution)/shard_map/reduce_scatter | solution.py:278
  (108 other events, 342.6 us)
Sparse Core Ops, SparseCore 0:
  9.6 364.5 all-gather.1
  423.2 989.4 reduce-scatter.13
  1417.1 67.1 reduce-scatter.7
  1488.9 128.1 reduce-scatter.5
  1621.1 163.4 reduce-scatter.9
  1788.6 162.5 reduce-scatter.11
where the time goes:
time: 1970 us; the launch traced here: 1960 us
  waiting for transfers between devices  1460 us (74%)
  matrix products  157 us (8%)
  blocking collectives  154 us (8%)
  other arithmetic  80.9 us (4%)
  local copies, waits for them, and re-layouts  65.4 us (3%)
  starting transfers between devices  28.1 us (1%)
    ppermute x14, waiting for transfers between devices, passed_along(): return lax.ppermute(block, axis, route)  383 us
    all_gather x1, waiting for transfers between devices, on_device(): lax.all_gather(probe_dirs, 'ex', axis=1, tiled=True)  345 us
    reduce_scatter x1, waiting for transfers between devices, on_device(): lax.psum_scatter(jnp.einsum('tc,tq->cq', columns, weighted, preferred_ele...  195 us
    reduce_scatter x1, waiting for transfers between devices, on_device(): lax.psum_scatter(grad_up_weight, 'ex', scatter_dimension=0, tiled=True)  168 us
    reduce_scatter x1, waiting for transfers between devices, on_device(): lax.psum_scatter(grad_down_weight, 'ex', scatter_dimension=0, tiled=True)  167 us
    psum x1, blocking collectives, on_device(): probe_scores, small_total = lax.psum((score_term, small_flat), 'ex')  154 us
    reduce_scatter x1, waiting for transfers between devices, on_device(): lax.psum_scatter(grad_qkv_weight, 'ex', scatter_dimension=0, tiled=True)  133 us
    reduce_scatter x1, waiting for transfers between devices, on_device(): lax.psum_scatter(grad_out_weight, 'ex', scatter_dimension=0, tiled=True)  66.6 us
  transfers between devices with their start and end apart: 20, of which 16 were waited for; matrix products, arithmetic and copies ran while one was open for 12% of the time, Pallas kernels for 0%

commit v1 on v0

v1 whole, which is shorter than its diff:
```python
import functools

import jax
import jax.numpy as jnp
import numpy as np
from jax import lax
from jax.experimental import pallas as pl
from jax.experimental.pallas import tpu as pltpu
from jax.sharding import PartitionSpec as P

HEADS = 12
HEAD_DIM = 64
ROT = 16
SEQ = 2048

BF = jnp.bfloat16
F32 = jnp.float32
eps_norm = 1e-05
masked_score = -1e30
half_root = 0.7071067811865476
gauss_peak = 0.3989422804014327
MB = 1024 * 1024
LANES = 128
LIGHT = pl.CostEstimate(flops=1000, bytes_accessed=1000, transcendentals=0)
BIG = 58


def dot(a, b):
    return jnp.dot(a, b, preferred_element_type=F32)


def dot_nt(a, b):
    return lax.dot_general(a, b, (((1,), (1,)), ((), ())), preferred_element_type=F32)


def dot_tn(a, b):
    return lax.dot_general(a, b, (((0,), (0,)), ((), ())), preferred_element_type=F32)


def spread_of(features):
    center = jnp.mean(features, axis=-1, keepdims=True)
    centred = features - center
    spread = jnp.mean(centred * centred, axis=-1, keepdims=True)
    return centred, lax.rsqrt(spread + eps_norm)


def standardize(features):
    centred, factor = spread_of(features)
    return centred * factor


def norm_input_term(grad, gain_row, unit, factor):
    unit_grad = grad * gain_row
    inner = unit_grad - jnp.mean(unit_grad, -1, keepdims=True)
    return (inner - unit * jnp.mean(unit_grad * unit, -1, keepdims=True)) * factor


def gelu_parts(pre_act):
    below = 0.5 + 0.5 * lax.erf(pre_act * half_root)
    density = gauss_peak * jnp.exp(-0.5 * pre_act * pre_act)
    return below, density


def rotary_tables(count):
    steps = np.arange(ROT // 2, dtype=np.float32) * np.float32(2.0 / ROT)
    inverse = np.power(np.float32(10000.0), -steps).astype(np.float32)
    angles = np.arange(count, dtype=np.float32)[:, None] * inverse[None, :]
    angles = np.concatenate([angles, angles], axis=1)
    cosine = np.ones((count, HEAD_DIM), np.float32)
    sine = np.zeros((count, HEAD_DIM), np.float32)
    cosine[:, :ROT], sine[:, :ROT] = np.cos(angles), np.sin(angles)
    return np.concatenate([cosine, cosine], axis=1), np.concatenate([sine, sine], axis=1)


def params(limit_mb, **more):
    return pltpu.CompilerParams(vmem_limit_bytes=limit_mb * MB, **more)


def shaped(shape, dtype):
    return jax.ShapeDtypeStruct(shape, dtype)


def whole(*shape):
    return pl.BlockSpec(shape, lambda i: (0,) * len(shape))


VMEM = pl.BlockSpec(memory_space=pltpu.VMEM)
SMEM = pl.BlockSpec(memory_space=pltpu.SMEM)
ANY = pl.BlockSpec(memory_space=pl.ANY)


def call(kernel, *, inputs, in_specs, after=(), aliases=None, **more):
    spare = len(after)

    def body(*refs):
        kernel(*refs[: len(inputs)], *refs[len(inputs) + spare :])

    return pl.pallas_call(
        body, in_specs=list(in_specs) + [ANY] * spare, input_output_aliases=aliases or {},
        cost_estimate=LIGHT, **more,
    )(*inputs, *after)


def tie(value, after):
    return call(
        lambda value_ref, out_ref: None,
        inputs=[value],
        after=after,
        aliases={0: 0},
        in_specs=[ANY],
        out_specs=ANY,
        out_shape=shaped(value.shape, value.dtype),
        name="tie",
    )


def pack_kernel(dirs_ref, packed_ref, sems):
    probes = dirs_ref.shape[0]
    blocks, _, width = packed_ref.shape
    part_width = width // probes
    copies = []
    for block in range(blocks):
        for k in range(probes):
            source = dirs_ref.at[k, :, block * part_width : (block + 1) * part_width]
            target = packed_ref.at[block, :, k * part_width : (k + 1) * part_width]
            copies.append(pltpu.make_async_copy(source, target, sems.at[len(copies)]))
    for copy in copies:
        copy.start()
    for copy in copies:
        copy.wait()


def pack(dirs, blocks, rows, after):
    probes, local_rows, hidden_width = dirs.shape
    part_width = hidden_width // blocks
    if rows > 1:
        split = dirs.reshape(probes, local_rows, rows, blocks, part_width // rows)
        return split.transpose(3, 1, 0, 2, 4).reshape(blocks, local_rows, probes * part_width)
    return call(
        pack_kernel,
        inputs=[dirs],
        after=after,
        in_specs=[ANY],
        out_specs=ANY,
        out_shape=shaped((blocks, local_rows, probes * part_width), dirs.dtype),
        scratch_shapes=[pltpu.SemaphoreType.DMA((blocks * probes,))],
        compiler_params=params(8),
        name="pack",
    )


def stack_kernel(plan, *refs):
    sources, targets = refs[: -len(plan)], refs[-len(plan) :]
    for parts, target in zip(plan, targets):
        number = 0
        for part in parts:
            count = sources[part].shape[0]
            target[number : number + count] = sources[part][...]
            number += count


def stack(sources, plan, after):
    heights = [sum(sources[part].shape[0] for part in parts) for parts in plan]
    return call(
        functools.partial(stack_kernel, plan),
        inputs=sources,
        after=after,
        in_specs=[VMEM] * len(sources),
        out_specs=[VMEM] * len(plan),
        out_shape=[shaped((n,) + sources[parts[0]].shape[1:], BF) for n, parts in zip(heights, plan)],
        compiler_params=params(8),
        name="stack",
    )


def vectors_kernel(*refs):
    *sources, first_bias, second_bias, vectors_ref = refs
    vectors_ref[...] = jnp.zeros_like(vectors_ref)
    for number, source in enumerate(sources):
        vectors_ref[number : number + 1, :] = source[...].reshape(1, -1)
    total = first_bias[...].astype(F32) + second_bias[...].astype(F32)
    vectors_ref[len(sources) : len(sources) + 1, :] = total.reshape(1, -1)


def vectors_of(*sources):
    return call(
        vectors_kernel,
        inputs=list(sources),
        in_specs=[VMEM] * len(sources),
        out_specs=VMEM,
        out_shape=shaped((8, sources[0].shape[0]), F32),
        compiler_params=params(4),
        name="vectors",
    )


def local_kernel(
    tokens_ref, grads_ref, up_ref, up_bias_ref, down_ref, vectors_ref,
    base_ref, rest_ref, small_ref, normed_s, branch_s, back_s,
):
    step = pl.program_id(0)
    gain, shift, out_bias = vectors_ref[2:3, :], vectors_ref[3:4, :], vectors_ref[4:5, :]

    @pl.when(step == 0)
    def _():
        unit = standardize(tokens_ref[...].astype(F32))
        normed_s[...] = (unit * gain + shift).astype(BF)
        branch_s[...] = jnp.zeros_like(branch_s)
        back_s[...] = jnp.zeros_like(back_s)

    bias = up_bias_ref[pl.ds(pl.multiple_of(step * up_ref.shape[1], LANES), up_ref.shape[1])]
    hidden = dot(normed_s[...], up_ref[...]) + bias.astype(F32).reshape(1, -1)
    upstream = dot_nt(grads_ref[...], down_ref[...])
    below, density = gelu_parts(hidden)
    branch_s[...] += dot((hidden * below).astype(BF), down_ref[...])
    hidden_grad = (upstream * (below + hidden * density)).astype(BF)
    back_s[...] += dot_nt(hidden_grad, up_ref[...])

    @pl.when(step == pl.num_programs(0) - 1)
    def _():
        inputs = tokens_ref[...].astype(F32)
        cot = grads_ref[...].astype(F32)
        centred, factor = spread_of(inputs)
        unit = centred * factor
        back = back_s[...]
        base_ref[...] = inputs + branch_s[...] + out_bias
        rest_ref[...] = cot + norm_input_term(back, gain, unit, factor)
        small_ref[...] = jnp.zeros_like(small_ref)
        small_ref[0:1, :] = jnp.sum(cot, axis=0, keepdims=True)
        small_ref[1:2, :] = jnp.sum(back * unit, axis=0, keepdims=True)
        small_ref[2:3, :] = jnp.sum(back, axis=0, keepdims=True)


def local_part(tokens, grads, up_weight, up_bias, down_weight, vectors):
    tok_count, feature_width = tokens.shape
    hidden_width = up_weight.shape[1]
    step = 512
    own = whole(tok_count, feature_width)
    return call(
        local_kernel,
        inputs=[tokens, grads, up_weight, up_bias, down_weight, vectors],
        grid=(hidden_width // step,),
        in_specs=[
            own, own,
            pl.BlockSpec((feature_width, step), lambda i: (0, i)),
            whole(hidden_width),
            pl.BlockSpec((step, feature_width), lambda i: (i, 0)),
            whole(8, feature_width),
        ],
        out_specs=[own, own, whole(8, feature_width)],
        out_shape=[
            shaped((tok_count, feature_width), F32),
            shaped((tok_count, feature_width), F32),
            shaped((8, feature_width), F32),
        ],
        scratch_shapes=[
            pltpu.VMEM((tok_count, feature_width), BF),
            pltpu.VMEM((tok_count, feature_width), F32),
            pltpu.VMEM((tok_count, feature_width), F32),
        ],
        compiler_params=params(BIG),
        name="local",
    )


def lanes(rows):
    return lax.broadcasted_iota(jnp.int32, (rows, 2 * HEAD_DIM), 1)


def flipped(tile):
    return pltpu.roll(tile, HEAD_DIM, 1)


def joined(left, right):
    return jnp.where(lanes(left.shape[0]) < HEAD_DIM, left, flipped(right))


def half_turned(tile):
    place_in = lanes(tile.shape[0]) % HEAD_DIM
    low = pltpu.roll(tile, 2 * HEAD_DIM - ROT // 2, 1)
    high = pltpu.roll(tile, ROT // 2, 1)
    return jnp.where(place_in < ROT // 2, -low, jnp.where(place_in < ROT, high, 0.0))


def with_column(tile, lane, column):
    first = column.astype(BF).astype(F32)
    number = lanes(tile.shape[0])
    return jnp.where(number == lane, first, jnp.where(number == lane + 1, column - first, tile))


def heads_joined(values):
    heads = len(values)
    values = [joined(values[k], values[k + 1]) if k + 1 < heads else values[k] for k in range(0, heads, 2)]
    if heads % 2:
        values[-1] = jnp.where(lanes(values[-1].shape[0]) < HEAD_DIM, values[-1], 0.0)
    return jnp.concatenate(values, axis=1)


def attention_kernel(heads, blocks, plan, *refs):
    count = sum(len(sides) for sides, _ in plan)
    piece_refs, refs = list(refs[:count]), refs[count:]
    groups = [(sides, distances, [piece_refs.pop(0) for _ in sides]) for sides, distances in plan]
    (
        place_ref, tokens_ref, weight_ref, bias_ref, vectors_ref, out_weight_ref, cos_ref, sin_ref, seg_ref,
        local_ref, up_bias_ref, shared_ref, keep_ref, send_ref,
        weight_s, bias_s, out_weight_s, attended_s, query_s, key_s, value_s, back_s,
        query_grad_s, key_grad_s, value_grad_s, grad_s, grad_out_s, small_s,
    ) = refs
    place = place_ref[0]
    block, feature_width = tokens_ref.shape
    pair = 2 * HEAD_DIM
    scale = HEAD_DIM ** (-0.5)
    gain, shift = vectors_ref[0:1, :], vectors_ref[1:2, :]
    own_rows = pl.ds(pl.multiple_of(place * block, block), block)

    def rows_of(number):
        return pl.ds(pl.multiple_of(number * block, block), block)

    def side_rows(distance, side, count):
        own = place_ref[1] % (block // count)
        first = jnp.bitwise_xor(place, distance) * block + jnp.bitwise_xor(own, side) * count
        return pl.ds(pl.multiple_of(first, count), count)

    def together(refs, slot, part):
        return jnp.concatenate([ref[slot, part] for ref in refs], axis=0)

    def arrange(source, target):
        for head in range(heads):
            start = head * 3 * HEAD_DIM
            tile = source[:, start : start + pair].astype(F32)
            target[:, head * pair : (head + 1) * pair] = tile.astype(target.dtype)
            target[:, (heads + head) * pair : (heads + head + 1) * pair] = half_turned(tile).astype(target.dtype)
        values = [source[:, (3 * head + 2) * HEAD_DIM : (3 * head + 3) * HEAD_DIM] for head in range(heads)]
        values.append(jnp.zeros((source.shape[0], -heads * HEAD_DIM % pair), source.dtype))
        target[:, 2 * heads * pair :] = jnp.concatenate(values, axis=1).astype(target.dtype)

    arrange(weight_ref, weight_s)
    arrange(bias_ref, bias_s)
    out_weight_s[...] = jnp.zeros_like(out_weight_s)
    out_weight_s[: heads * HEAD_DIM, :] = out_weight_ref[...]

    def project(sides, refs, slot, distance):
        unit = standardize(together(refs, slot, 0).astype(F32))
        normed = (unit * gain + shift).astype(BF)
        whole_part = dot(normed, weight_s[...]) + bias_s[:1, :]
        whole_back = dot_nt(together(refs, slot, 1), out_weight_s[...])
        count = block // len(sides)
        for number, side in enumerate(sides):
            here = slice(number * count, (number + 1) * count)
            place_heads(side_rows(distance, side, count), whole_part[here], whole_back[here])

    def place_heads(rows, part, back_part):
        cosine, sine = cos_ref[rows, :], sin_ref[rows, :]
        number = lanes(part.shape[0])
        segment = seg_ref[rows, :]
        match = (number == HEAD_DIM + segment // 8) | (number == HEAD_DIM + 8 + segment % 8)
        coded = (number >= HEAD_DIM) & (number < HEAD_DIM + 16)
        query_code = jnp.where(coded & ~match, masked_score, 0.0)
        ones = (number >= HEAD_DIM + 16) & (number < HEAD_DIM + 18)
        key_code = jnp.where(match | ones, 1.0, 0.0)
        value_code = jnp.where((number >= HEAD_DIM) & (number < HEAD_DIM + 2), 1.0, 0.0)
        first = number < HEAD_DIM
        for head in range(heads):
            plain = part[:, head * pair : (head + 1) * pair]
            turned = part[:, (heads + head) * pair : (heads + head + 1) * pair]
            both = plain * cosine + turned * sine
            query_s[head, rows, :] = jnp.where(first, both * scale, query_code).astype(BF)
            key_s[head, rows, :] = jnp.where(first, flipped(both), key_code).astype(BF)
            start = 2 * heads * pair + head // 2 * pair
            tile = part[:, start : start + pair]
            back_tile = back_part[:, head // 2 * pair : head // 2 * pair + pair]
            if head % 2:
                tile, back_tile = flipped(tile), flipped(back_tile)
            value_s[head, rows, :] = jnp.where(first, tile, value_code).astype(BF)
            back_s[head, rows, :] = jnp.where(first, back_tile, 0.0).astype(BF)

    for sides, distances, refs in groups:
        for slot, distance in enumerate(distances):
            project(sides, refs, slot, distance)

    square = (block, block)
    lower = lax.broadcasted_iota(jnp.int32, square, 1) <= lax.broadcasted_iota(jnp.int32, square, 0)

    def attend(head, carry):
        def scores_of(number):
            start, stop = number * block, (number + 1) * block
            query = query_s[head, start:stop, :]
            near = jnp.where(lower, dot_nt(query, key_s[head, start:stop, :]), masked_score)
            return near, dot_nt(query, key_s[head, :start, :]) if number else None

        ahead = scores_of(0)
        for number in range(blocks):
            start, stop = number * block, (number + 1) * block
            near, far = ahead
            if number + 1 < blocks:
                ahead = scores_of(number + 1)
            top = jnp.max(near, axis=-1, keepdims=True)
            if number:
                top = jnp.maximum(top, jnp.max(far, axis=-1, keepdims=True))
            got = dot(jnp.exp(near - top).astype(BF), value_s[head, start:stop, :])
            if number:
                got = got + dot(jnp.exp(far - top).astype(BF), value_s[head, :start, :])
            total = got[:, HEAD_DIM : HEAD_DIM + 1]
            attended = got / total
            attended_s[head, start:stop, :] = attended.astype(BF)
            back = back_s[head, start:stop, :].astype(F32)
            delta = jnp.sum(attended * back, axis=-1, keepdims=True)
            log_total = top + jnp.log(total)
            query = query_s[head, start:stop, :].astype(F32)
            query_s[head, start:stop, :] = with_column(query, HEAD_DIM + 16, -log_total).astype(BF)
            back_s[head, start:stop, :] = with_column(back, HEAD_DIM, -delta).astype(BF)
        return carry

    lax.fori_loop(0, heads, attend, 0)

    def joined_rows(rows):
        return heads_joined([attended_s[head, rows, :].astype(F32) for head in range(heads)]).astype(BF)

    shared_ref[:block, feature_width:] = joined_rows(own_rows)[:, : heads * HEAD_DIM]

    total = jnp.zeros((out_weight_s.shape[0], feature_width), F32)
    for sides, distances, refs in groups:
        for slot, distance in enumerate(distances):
            rows = [joined_rows(side_rows(distance, side, block // len(sides))) for side in sides]
            total = total + dot_tn(jnp.concatenate(rows, axis=0), together(refs, slot, 1))
    grad_out_s[...] = total

    square = (block, block)
    lower = lax.broadcasted_iota(jnp.int32, square, 1) <= lax.broadcasted_iota(jnp.int32, square, 0)
    upper = lax.broadcasted_iota(jnp.int32, square, 0) <= lax.broadcasted_iota(jnp.int32, square, 1)

    def to_keys(rows, head, mask):
        query, back = query_s[head, rows, :], back_s[head, rows, :]
        scores = dot_nt(key_s[head, own_rows, :], query)
        if mask is not None:
            scores = jnp.where(mask, scores, masked_score)
        probs = jnp.exp(scores)
        score_grad = probs * dot_nt(value_s[head, own_rows, :], back)
        return dot(probs.astype(BF), back), dot(score_grad.astype(BF), query)

    def to_queries(rows, head, mask):
        key, value = key_s[head, rows, :], value_s[head, rows, :]
        scores = dot_nt(query_s[head, own_rows, :], key)
        if mask is not None:
            scores = jnp.where(mask, scores, masked_score)
        score_grad = jnp.exp(scores) * dot_nt(back_s[head, own_rows, :], value)
        return dot(score_grad.astype(BF), key)

    for head in range(heads):
        value_grad_s[head], key_grad_s[head] = to_keys(own_rows, head, upper)
        query_grad_s[head] = to_queries(own_rows, head, lower)

    def later(number, carry):
        rows = rows_of(number)
        for head in range(heads):
            value_grad, key_grad = to_keys(rows, head, None)
            value_grad_s[head] += value_grad
            key_grad_s[head] += key_grad
        return carry

    def earlier(number, carry):
        rows = rows_of(number)
        for head in range(heads):
            query_grad_s[head] += to_queries(rows, head, None)
        return carry

    lax.fori_loop(place + 1, blocks, later, 0)
    lax.fori_loop(0, place, earlier, 0)

    cosine, sine = cos_ref[own_rows, :], sin_ref[own_rows, :]
    tiles = []
    for head in range(heads):
        both = joined(query_grad_s[head] * scale, key_grad_s[head])
        both = both * cosine - half_turned(both * sine)
        value = value_grad_s[head]
        if head % 2 == 0:
            tiles += [both, value]
        else:
            tiles[-1] = joined(tiles[-1], both)
            tiles.append(joined(flipped(both), value))
    if heads % 2:
        tiles[-1] = jnp.where(lanes(block) < HEAD_DIM, tiles[-1], 0.0)
    mixed_grad = jnp.concatenate(tiles, axis=1).astype(BF)[:, : 3 * heads * HEAD_DIM]
    unit = standardize(tokens_ref[...].astype(F32))
    normed = (unit * gain + shift).astype(BF)
    normed_back = dot_nt(mixed_grad, weight_ref[...])
    shared_ref[:block, :feature_width] = normed_back.astype(BF)

    local_rows = feature_width // blocks
    holds, first = place_ref[2] == 1, pl.multiple_of(place_ref[3], local_rows)
    rows = jnp.where(holds, grad_out_s[pl.ds(first, local_rows), :], 0.0)
    shared_ref[block:, :feature_width] = rows.astype(BF)
    shared_ref[block:, feature_width:] = jnp.zeros((local_rows, heads * HEAD_DIM), BF)

    width = keep_ref.shape[2]
    grad_qkv = dot_tn(normed, mixed_grad).astype(BF)
    fill = jnp.zeros((feature_width, width - grad_qkv.shape[1]), BF)
    grad_s[...] = jnp.concatenate([grad_qkv, fill], axis=1).reshape(grad_s.shape)
    bit = place % 2
    for number in range(blocks // 2):
        keep_ref[number] = grad_s[2 * number + bit]
        send_ref[number * local_rows : (number + 1) * local_rows, :] = grad_s[2 * number + 1 - bit]

    piece = feature_width // 2
    probe_place = place_ref[1]
    sole = probe_place == 0
    small_s[...] = jnp.zeros_like(small_s)

    def put(row, values):
        small_s[row : row + 1, :piece] = values[:, :piece]
        small_s[row + 1 : row + 2, :piece] = values[:, piece:]

    for number in range(3):
        put(2 * number, jnp.where(sole, local_ref[number : number + 1, :], 0.0))
    put(6, jnp.sum(normed_back * unit, axis=0, keepdims=True))
    put(8, jnp.sum(normed_back, axis=0, keepdims=True))
    bias_grad = jnp.sum(mixed_grad.astype(F32), axis=0, keepdims=True)
    small_s[pl.ds(10 + 2 * probe_place, 1), :piece] = bias_grad[:, :piece]
    rest = bias_grad.shape[1] - piece
    small_s[pl.ds(11 + 2 * probe_place, 1), :rest] = bias_grad[:, piece:]
    small_s[pl.ds(10 + 2 * place_ref[4] + place, 1), :piece] = jnp.where(sole, up_bias_ref[...], 0.0)
    put_small(send_ref, blocks // 2 * local_rows, small_s[...])


def put_small(target, first, small):
    count = small.shape[0]
    high = small.astype(BF)
    target[first : first + count, : small.shape[1]] = high
    target[first + count : first + 2 * count, : small.shape[1]] = (small - high.astype(F32)).astype(BF)


def get_small(source, first, width):
    count = (source.shape[0] - first) // 2
    high = source[first : first + count, :width].astype(F32)
    return high + source[first + count :, :width].astype(F32)


def fold_kernel(place_ref, keep_ref, mine_ref, got_ref, *refs):
    count, local_rows, width = keep_ref.shape
    send_ref, total_s = refs[-2:]
    for number in range(count):
        got = got_ref[number * local_rows : (number + 1) * local_rows, :].astype(F32)
        total_s[number] = (keep_ref[number].astype(F32) + got).astype(BF)
    bit = place_ref[0]
    for number in range(count // 2):
        refs[0][number] = total_s[2 * number + bit]
        send_ref[number * local_rows : (number + 1) * local_rows, :] = total_s[2 * number + 1 - bit]
    if count == 1:
        send_ref[:local_rows, :] = total_s[0]
    small = get_small(mine_ref, count * local_rows, width) + get_small(got_ref, count * local_rows, width)
    put_small(send_ref, max(count // 2, 1) * local_rows, small)


def fold(bit, keep, mine, got, after):
    count, local_rows, width = keep.shape
    left = max(count // 2, 1) * local_rows + mine.shape[0] - count * local_rows
    halves = [shaped((count // 2, local_rows, width), BF)] if count > 1 else []
    return call(
        fold_kernel,
        inputs=[bit[None].astype(jnp.int32), keep, mine, got],
        after=after,
        in_specs=[SMEM] + [VMEM] * 3,
        out_specs=[VMEM] * (len(halves) + 1),
        out_shape=halves + [shaped((left, width), BF)],
        scratch_shapes=[pltpu.VMEM(keep.shape, BF)],
        compiler_params=params(8),
        name="fold",
    )


def pair_kernel(local_rows, place_ref, mine_ref, got_ref, out_ref):
    width = mine_ref.shape[1]
    odd = place_ref[0] == 1
    mine, got = mine_ref[:local_rows, :], got_ref[:local_rows, :]
    out_ref[:local_rows, :width] = jnp.where(odd, got, mine)
    out_ref[:local_rows, width:] = jnp.where(odd, mine, got)
    put_small(out_ref, local_rows, get_small(mine_ref, local_rows, width) + get_small(got_ref, local_rows, width))
    out_ref[local_rows:, width:] = jnp.zeros((out_ref.shape[0] - local_rows, width), BF)


def pair(core, mine, got, local_rows, after):
    return call(
        functools.partial(pair_kernel, local_rows),
        inputs=[core[None].astype(jnp.int32), mine, got],
        after=after,
        in_specs=[SMEM, VMEM, VMEM],
        out_specs=VMEM,
        out_shape=shaped((mine.shape[0], 2 * mine.shape[1]), BF),
        compiler_params=params(8),
        name="pair",
    )


def join_kernel(local_rows, mixed_width, blocks, place_ref, mine_ref, got_ref, qkv_ref, *vector_refs):
    *sum_refs, qkv_bias_ref, up_bias_ref = vector_refs
    width = mine_ref.shape[1] // 2
    upper = place_ref[0] == 1
    mine, got = mine_ref[:local_rows, :], got_ref[:local_rows, :]
    parts = []
    for side in (jnp.where(upper, got, mine), jnp.where(upper, mine, got)):
        parts += [side[:, :mixed_width], side[:, width : width + mixed_width]]
    qkv_ref[...] = jnp.concatenate([part.astype(F32) for part in parts], axis=1)
    small = get_small(mine_ref, local_rows, width) + get_small(got_ref, local_rows, width)
    piece = sum_refs[0].shape[0] // 2

    def rows(first, count, total):
        parts = [small[number : number + 1, :piece] for number in range(first, first + count)]
        return jnp.concatenate(parts, axis=1)[:, :total]

    for number, ref in enumerate(sum_refs):
        ref[...] = rows(2 * number, 2, 2 * piece).reshape(ref.shape)
    groups = qkv_bias_ref.shape[0] // mixed_width
    first = 2 * len(sum_refs)
    bias = [rows(first + 2 * number, 2, mixed_width) for number in range(groups)]
    qkv_bias_ref[...] = jnp.concatenate(bias, axis=1).reshape(qkv_bias_ref.shape)
    up_bias_ref[...] = rows(first + 2 * groups, blocks, blocks * piece).reshape(up_bias_ref.shape)


def join(upper, mine, got, local_rows, mixed_width, blocks, feature_width, after):
    vector = shaped((feature_width,), F32)
    return call(
        functools.partial(join_kernel, local_rows, mixed_width, blocks),
        inputs=[upper[None].astype(jnp.int32), mine, got],
        after=after,
        in_specs=[SMEM, VMEM, VMEM],
        out_specs=[VMEM] * 8,
        out_shape=[shaped((local_rows, 4 * mixed_width), F32)]
        + [vector] * 5
        + [shaped((4 * mixed_width,), F32), shaped((blocks * (feature_width // 2),), F32)],
        compiler_params=params(12),
        name="join",
    )


def attention(
    heads, blocks, numbers, pieces, tokens, weight, bias, vectors, out_weight, segments, local_small, up_bias, after
):
    tok_count, feature_width = tokens.shape
    pair = 2 * HEAD_DIM
    head_width = heads * HEAD_DIM
    mixed_width = 3 * head_width
    value_tiles = -(-heads // 2) * pair
    cos_table, sin_table = rotary_tables(SEQ)
    local_rows = feature_width // blocks
    width = -(-mixed_width // LANES) * LANES
    small_rows = -(-(10 + 2 * HEADS // heads + blocks) // 16) * 16
    return call(
        functools.partial(attention_kernel, heads, blocks, [plan for _, plan in pieces]),
        inputs=[array for arrays, _ in pieces for array in arrays] + [
            numbers, tokens, weight,
            jnp.broadcast_to(bias.astype(F32)[None], (8, bias.shape[0])), vectors,
            out_weight, cos_table, sin_table, segments[:, None], local_small, up_bias,
        ],
        after=after,
        in_specs=[VMEM] * sum(len(arrays) for arrays, _ in pieces) + [SMEM] + [VMEM] * 10,
        out_specs=[VMEM] * 3,
        out_shape=[
            shaped((tok_count + local_rows, feature_width + head_width), BF),
            shaped((blocks // 2, local_rows, width), BF),
            shaped((blocks // 2 * local_rows + 2 * small_rows, width), BF),
        ],
        scratch_shapes=[
            pltpu.VMEM((feature_width, 2 * heads * pair + value_tiles), BF),
            pltpu.VMEM((8, 2 * heads * pair + value_tiles), F32),
            pltpu.VMEM((value_tiles, feature_width), BF),
        ]
        + [pltpu.VMEM((heads, SEQ, pair), BF)] * 5
        + [pltpu.VMEM((heads, tok_count, pair), F32)] * 3
        + [
            pltpu.VMEM((blocks, local_rows, width), BF),
            pltpu.VMEM((value_tiles, feature_width), F32),
            pltpu.VMEM((small_rows, width), F32),
        ],
        compiler_params=params(50),
        name="attention",
    )


def hidden_kernel(first_call, *refs):
    if first_call:
        grad_down_in, grad_up_in, bias_grad_in = (None, None, None)
    else:
        grad_down_in, grad_up_in, bias_grad_in = refs[-9:-6]
        refs = refs[:-9] + refs[-6:]
    piece_refs, (up_ref, up_bias_ref, down_ref, vectors_ref) = refs[1:-10], refs[-10:-6]
    normed_ref, turned_ref, curve_ref, grad_down_ref, grad_up_ref, bias_grad_ref = refs[-6:]
    cot = jnp.concatenate([ref[0, 1] for ref in piece_refs], axis=0)
    unit = standardize(jnp.concatenate([ref[0, 0] for ref in piece_refs], axis=0).astype(F32))
    normed = (unit * vectors_ref[2:3, :] + vectors_ref[3:4, :]).astype(BF)
    normed_ref[...] = normed
    turned = normed.T
    turned_ref[...] = turned
    hidden = dot(normed, up_ref[...]) + up_bias_ref[...]
    upstream = dot_nt(cot, down_ref[...])
    below, density = gelu_parts(hidden)
    active = (hidden * below).astype(BF)
    hidden_grad = (upstream * (below + hidden * density)).astype(BF)
    curve_ref[...] = upstream * density * (2.0 - hidden * hidden)

    @pl.when(pl.program_id(0) == 0)
    def _():
        for before, target in (
            (grad_down_in, grad_down_ref), (grad_up_in, grad_up_ref), (bias_grad_in, bias_grad_ref),
        ):
            target[...] = jnp.zeros_like(target) if first_call else before[...]

    grad_down_ref[...] += dot_tn(active, cot)
    grad_up_ref[...] += dot(turned, hidden_grad)
    bias_grad_ref[...] += jnp.sum(hidden_grad.astype(F32), axis=0, keepdims=True)


def hidden_units(place, pieces, up_part, up_bias_part, down_part, vectors, before):
    arrays = [array for arrays, _ in pieces for array in arrays]
    slots, _, side_rows, feature_width = arrays[0].shape
    part_width = up_bias_part.shape[1]
    tok_count = len(arrays) * side_rows
    count = slots * tok_count

    def fixed(*shape):
        return pl.BlockSpec(shape, lambda i, place_ref: (0,) * len(shape))

    piece = pl.BlockSpec((1, 2, side_rows, feature_width), lambda i, place_ref: (i, 0, 0, 0))
    sums = [fixed(part_width, feature_width), fixed(feature_width, part_width), fixed(1, part_width)]
    return pl.pallas_call(
        functools.partial(hidden_kernel, before is None),
        grid_spec=pltpu.PrefetchScalarGridSpec(
            num_scalar_prefetch=1,
            grid=(slots,),
            in_specs=[piece] * len(arrays) + [
                pl.BlockSpec((feature_width, part_width), lambda i, place_ref: (0, place_ref[0])),
                fixed(1, part_width),
                pl.BlockSpec((part_width, feature_width), lambda i, place_ref: (place_ref[0], 0)),
                fixed(8, feature_width),
            ] + (sums if before else []),
            out_specs=[
                pl.BlockSpec((tok_count, feature_width), lambda i, place_ref: (i, 0)),
                pl.BlockSpec((feature_width, tok_count), lambda i, place_ref: (0, i)),
                pl.BlockSpec((tok_count, part_width), lambda i, place_ref: (i, 0)),
            ] + sums,
        ),
        out_shape=[
            shaped((count, feature_width), BF),
            shaped((feature_width, count), BF),
            shaped((count, part_width), F32),
            shaped((part_width, feature_width), F32),
            shaped((feature_width, part_width), F32),
            shaped((1, part_width), F32),
        ],
        compiler_params=params(BIG),
        name="hidden_units",
        cost_estimate=LIGHT,
    )(
        jnp.where(up_part.shape[1] > part_width, place, 0)[None].astype(jnp.int32),
        *arrays, up_part, up_bias_part, down_part, vectors, *(before[3:] if before else []),
    )


def share_kernel(probes, place_ref, dirs_ref, grad_up_ref, share_ref):
    blocks, local_rows, width = share_ref.shape
    part_width = grad_up_ref.shape[1]
    half = part_width // 2
    grad_up = grad_up_ref[...]
    own = jnp.where(place_ref[0] == 1, grad_up[:, half:], grad_up[:, :half]).astype(BF)
    row = lax.broadcasted_iota(jnp.int32, (1, width - half), 1)
    scores = jnp.zeros((1, width - half), F32)
    for number in range(probes):
        part = dirs_ref[:, number * part_width : (number + 1) * part_width].astype(F32)
        score = jnp.sum(jnp.sum(part * grad_up, axis=0, keepdims=True), axis=1, keepdims=True)
        high = score.astype(BF).astype(F32)
        scores = jnp.where(row == number, high, scores)
        scores = jnp.where(row == probes + number, score - high, scores)
    scores = jnp.broadcast_to(scores, (own.shape[0], width - half)).astype(BF)
    share_ref[...] = jnp.concatenate([own, scores], axis=1).reshape(share_ref.shape)


def share_of(core, dirs, grad_up, blocks, probes):
    feature_width, part_width = grad_up.shape
    width = -(-(part_width // 2 + 2 * probes) // LANES) * LANES
    return call(
        functools.partial(share_kernel, probes),
        inputs=[core[None].astype(jnp.int32), dirs, grad_up],
        in_specs=[SMEM, VMEM, VMEM],
        out_specs=VMEM,
        out_shape=shaped((blocks, feature_width // blocks, width), BF),
        compiler_params=params(16),
        name="share",
    )


def curvature_kernel(probes, halves, dirs_ref, *refs):
    token_refs, share_ref, (curvature_ref, total_s) = refs[: 3 * halves], refs[3 * halves], refs[-2:]
    step = pl.program_id(0)
    width = dirs_ref.shape[1]
    part_width = width // probes

    @pl.when(step == 0)
    def _():
        total_s[...] = jnp.zeros_like(total_s)

    for number in range(halves):
        normed_ref, turned_ref, curve_ref = token_refs[3 * number : 3 * number + 3]
        along = dot(normed_ref[...], dirs_ref[...])
        curve = curve_ref[...]
        weighted = []
        for k in range(probes):
            part = along[:, k * part_width : (k + 1) * part_width]
            weighted.append((part * curve).astype(BF))
        total_s[...] += dot(turned_ref[...], jnp.concatenate(weighted, axis=1))

    @pl.when(step == pl.num_programs(0) - 1)
    def _():
        curvature_ref[:, :, :width] = total_s[...].astype(BF).reshape(curvature_ref.shape[:2] + (width,))
        if curvature_ref.shape[2] > width:
            curvature_ref[:, :, width:] = share_ref[...]


def curvature_part(blocks, number, probes, halves, dirs, share, after):
    normed, _, curve = halves[0]
    (count, feature_width), part_width = normed.shape, curve.shape[1]
    width = probes * part_width
    steps = 2
    tok_count = count // steps
    more = ([], [], 0) if share is None else ([whole(*share.shape)], [share], share.shape[2])
    out = (blocks, feature_width // blocks, width + more[2])
    return call(
        functools.partial(curvature_kernel, probes, len(halves)),
        inputs=[dirs] + [array for half in halves for array in half] + more[1],
        after=after,
        grid=(steps,),
        in_specs=[pl.BlockSpec((feature_width, width), lambda i: (0, number))]
        + [
            pl.BlockSpec((tok_count, feature_width), lambda i: (i, 0)),
            pl.BlockSpec((feature_width, tok_count), lambda i: (0, i)),
            pl.BlockSpec((tok_count, part_width), lambda i: (i, 0)),
        ] * len(halves)
        + more[0],
        out_specs=whole(*out),
        out_shape=shaped(out, BF),
        scratch_shapes=[pltpu.VMEM((feature_width, width), F32)],
        compiler_params=params(BIG),
        name="curvature",
    )


def unpack_kernel(probes, share, got_ref, *refs):
    blocks, _, width = got_ref.shape
    part_width = (width - share) // probes
    curvature_ref = refs[-3] if share else refs[-1]
    number = pl.program_id(0)
    for block in range(blocks):
        here = slice(block * part_width, (block + 1) * part_width)
        for k in range(probes):
            @pl.when(number == k)
            def _(k=k):
                part = got_ref[block, :, k * part_width : (k + 1) * part_width]
                curvature_ref[0, :, here] = part.astype(F32)
    if share:
        up_ref, score_ref = refs[-2:]

        @pl.when(number == 0)
        def _():
            total = jnp.zeros(score_ref.shape, F32)
            for block in range(blocks):
                part = got_ref[block, :, width - share :]
                up_ref[:, block * share : (block + 1) * share] = part
                total = total + part[: total.shape[0], share - LANES :].astype(F32)
            score_ref[...] = total


def unpack(got, number, probes, share, probe_count, before, after):
    blocks, local_rows, width = got.shape
    part_width = (width - share) // probes
    out_specs = [pl.BlockSpec((1, local_rows, blocks * part_width), lambda i: (number * probes + i, 0, 0))]
    out_shape = [shaped((probe_count, local_rows, blocks * part_width), F32)]
    if share:
        out_specs += [whole(local_rows, blocks * share), whole(16, LANES)]
        out_shape += [shaped((local_rows, blocks * share), BF), shaped((16, LANES), F32)]
    return call(
        functools.partial(unpack_kernel, probes, share),
        inputs=[got],
        after=[*([] if before is None else [before]), *after],
        aliases={1: 0} if before is not None else {},
        grid=(probes,),
        in_specs=[whole(*got.shape)],
        out_specs=out_specs,
        out_shape=out_shape,
        compiler_params=params(BIG),
        name="unpack",
    )


def spread_kernel(blocks, half, place_ref, mine_ref, got_ref, out_ref):
    odd = place_ref[0] == 1
    stride = mine_ref.shape[1] // blocks
    for block in range(blocks):
        here = slice(block * stride, block * stride + half)
        mine, got = mine_ref[:, here], got_ref[:, here]
        both = jnp.concatenate([jnp.where(odd, got, mine), jnp.where(odd, mine, got)], axis=1)
        out_ref[:, block * 2 * half : (block + 1) * 2 * half] = both.astype(F32)


def spread(core, mine, got, blocks, half):
    return call(
        functools.partial(spread_kernel, blocks, half),
        inputs=[core[None].astype(jnp.int32), mine, got],
        in_specs=[SMEM, VMEM, VMEM],
        out_specs=VMEM,
        out_shape=shaped((mine.shape[0], blocks * 2 * half), F32),
        compiler_params=params(12),
        name="spread",
    )


def merge_kernel(tok_count, feature_width, place_ref, mine_ref, got_ref, merged_ref):
    odd = place_ref[0] == 1
    total = mine_ref[:, :feature_width].astype(F32) + got_ref[:, :feature_width].astype(F32)
    merged_ref[:, :feature_width] = total.astype(BF)
    mine, got = mine_ref[:, feature_width:], got_ref[:, feature_width:]
    merged_ref[:, feature_width:] = jnp.concatenate(
        [jnp.where(odd, got, mine), jnp.where(odd, mine, got)], axis=1
    )


def merge(core, mine, got, tok_count, feature_width):
    count, width = mine.shape
    return call(
        functools.partial(merge_kernel, tok_count, feature_width),
        inputs=[core[None].astype(jnp.int32), mine, got],
        in_specs=[SMEM, VMEM, VMEM],
        out_specs=VMEM,
        out_shape=shaped((count, 2 * width - feature_width), BF),
        compiler_params=params(12),
        name="merge",
    )


def finish_kernel(
    place_ref, mine_ref, got_ref, tokens_ref, base_ref, rest_ref, vectors_ref, out_weight_ref,
    layer_out_ref, input_grad_ref, grad_out_ref,
):
    tok_count, feature_width = tokens_ref.shape
    upper = place_ref[0] == 1
    mine, got = mine_ref[:tok_count, feature_width:], got_ref[:tok_count, feature_width:]
    attended = jnp.concatenate([jnp.where(upper, got, mine), jnp.where(upper, mine, got)], axis=1)
    layer_out_ref[...] = (base_ref[...] + dot(attended, out_weight_ref[...])).astype(BF)
    total = mine_ref[:, :feature_width].astype(F32) + got_ref[:, :feature_width].astype(F32)
    centred, factor = spread_of(tokens_ref[...].astype(F32))
    term = norm_input_term(total[:tok_count], vectors_ref[0:1, :], centred * factor, factor)
    input_grad_ref[...] = (rest_ref[...] + term).astype(BF)
    grad_out_ref[...] = total[tok_count:]


def finish(upper, mine, got, tokens, base, rest, vectors, out_weight, after):
    tok_count, feature_width = tokens.shape
    return call(
        finish_kernel,
        inputs=[upper[None].astype(jnp.int32), mine, got, tokens, base, rest, vectors, out_weight],
        after=after,
        in_specs=[SMEM] + [VMEM] * 7,
        out_specs=[VMEM] * 3,
        out_shape=[
            shaped(tokens.shape, BF),
            shaped(tokens.shape, BF),
            shaped((mine.shape[0] - tok_count, feature_width), F32),
        ],
        compiler_params=params(20),
        name="finish",
    )


def on_device(
    tokens,
    segment_ids,
    qkv_weight,
    qkv_bias,
    out_weight,
    out_bias,
    up_weight,
    up_bias,
    down_weight,
    down_bias,
    norm1_gain,
    norm1_bias,
    norm2_gain,
    norm2_bias,
    probe_dirs,
    out_grad,
):
    tok_count, feature_width = tokens.shape
    hidden_width = up_weight.shape[1]
    probe_count, local_rows = probe_dirs.shape[:2]
    groups = lax.axis_size("ex")
    probe_groups = lax.axis_size("probe")
    blocks = SEQ // tok_count
    rows = groups // blocks
    ex_place = lax.axis_index("ex")
    place = ex_place % blocks
    row_place = ex_place // blocks
    probe_place = lax.axis_index("probe")
    core, upper = probe_place % 2, probe_place // 2
    heads = HEADS // probe_groups
    head_width = heads * HEAD_DIM
    part_width = hidden_width // blocks
    fine = part_width // rows
    row_groups = None
    if rows > 1:
        row_groups = [[r * blocks + b for b in range(blocks)] for r in range(rows)]
    across = [[r * blocks + b for r in range(rows)] for b in range(blocks)]

    def swap(value, distance):
        return lax.ppermute(value, "ex", [(i, i ^ distance) for i in range(groups)])

    def swap_probe(value, distance):
        return lax.ppermute(value, "probe", [(i, i ^ distance) for i in range(probe_groups)])

    def over_rows(value):
        if rows > 1:
            return lax.psum_scatter(value, "ex", axis_index_groups=across, scatter_dimension=0, tiled=True)
        return value

    def my_part(value, axis):
        shape = value.shape
        split = shape[:axis] + (rows, blocks, fine) + shape[axis + 1 :]
        part = lax.dynamic_index_in_dim(value.reshape(split), place, axis + 1, keepdims=False)
        return part.reshape(shape[:axis] + (part_width,) + shape[axis + 1 :])

    half, quarter = tok_count // 2, tok_count // 4
    both = jnp.stack([tokens, out_grad])[None]
    mine = lax.dynamic_slice_in_dim(both, core * half, half, axis=2)
    share = lax.dynamic_slice_in_dim(both, probe_place * quarter, quarter, axis=2)
    near, aside, diagonal = swap(mine, 2), swap(mine, 1), swap(mine, 3)
    far, farthest = swap(share, 4), swap(share, 6)

    vectors = vectors_of(norm1_gain, norm1_bias, norm2_gain, norm2_bias, out_bias, down_bias)
    base, rest, local_small = local_part(tokens, out_grad, up_weight, up_bias, down_weight, vectors)

    first, second, third = stack(
        [mine, aside, near, diagonal, far, farthest], [(0, 1), (2, 3), (4, 5)], [local_small]
    )
    first_other, second_other = swap_probe(first, 1), swap_probe(second, 1)
    third_aside, third_over = swap(third, 1), swap_probe(third, 2)
    up_bias_part = my_part(up_bias, 0).astype(F32)[None]
    up_part, down_part = up_weight, down_weight
    if rows > 1:
        up_part, down_part = my_part(up_weight, 1), my_part(down_weight, 0)
    pieces = [
        ((first, first_other), ((0, 1), (0, 1))),
        ((second, second_other), ((0, 1), (2, 3))),
    ]
    units = hidden_units(place, pieces, up_part, up_bias_part, down_part, vectors, None)
    third_across = swap_probe(third_aside, 2)

    dirs = pack(probe_dirs, blocks, rows, [third_aside])
    dirs = lax.all_to_all(dirs, "ex", 0, 0, axis_index_groups=row_groups, tiled=True)
    dirs = dirs.reshape(blocks * local_rows, probe_count * part_width)
    if rows > 1:
        dirs = lax.all_gather(dirs, "ex", axis_index_groups=across, tiled=True)

    quarters = [third, third_over, third_aside, third_across]
    (quarters_all,) = stack(quarters, [(0, 1, 2, 3)], [units[5]])
    swapped = swap_probe(quarters_all, 1)
    swapped = [swapped[2 * k : 2 * k + 2] for k in range(4)]
    sides = (0, 2, 1, 3)
    pieces += [
        ((third, third_over, swapped[0], swapped[1]), (sides, (4, 6))),
        ((third_aside, third_across, swapped[2], swapped[3]), (sides, (5, 7))),
    ]
    halves = [units[:3]]
    units = hidden_units(place, pieces[2:], up_part, up_bias_part, down_part, vectors, units)
    halves.append(units[:3])
    grad_down, grad_up, grad_up_bias = units[3:]

    first_unit = probe_place * 3 * head_width
    block_rows = feature_width // blocks
    offset = place * block_rows - probe_place * head_width
    holds = (offset >= 0) & (offset < head_width)
    numbers = jnp.stack([place, probe_place, holds, jnp.where(holds, offset, 0), probe_groups])
    shared, keep, send = attention(
        heads, blocks, numbers.astype(jnp.int32), pieces, tokens,
        lax.dynamic_slice_in_dim(qkv_weight, first_unit, 3 * head_width, 1),
        lax.dynamic_slice_in_dim(qkv_bias, first_unit, 3 * head_width, 0), vectors,
        lax.dynamic_slice_in_dim(out_weight, probe_place * head_width, head_width, 0),
        lax.dynamic_slice_in_dim(segment_ids, row_place * SEQ, SEQ), local_small, grad_up_bias, [],
    )
    got = swap(send, 1)
    close = swap_probe(shared, 1)

    def to_owners(part):
        part = over_rows(part.reshape(feature_width, -1)).reshape(blocks, local_rows, -1)
        return lax.all_to_all(part, "ex", 0, 0, axis_index_groups=row_groups, tiled=True)

    chunk = probe_count // 2
    part = curvature_part(blocks, 0, chunk, halves, dirs, None, [shared])
    shared = merge(core, shared, close, tok_count, feature_width)
    close = swap_probe(shared, 2)
    keep, send = fold((place // 2) % 2, keep, send, got, [part])
    got = swap(send, 2)
    outgoing = [to_owners(tie(part, [send, shared]))]
    share = share_of(core, dirs, grad_up, blocks, probe_count)
    part = curvature_part(blocks, 1, chunk, halves, dirs, share, [send])
    layer_out, input_grad, grad_out_weight = finish(
        upper, shared, close, tokens, base, rest, vectors, out_weight, [part]
    )
    keep, send = fold((place // 4) % 2, keep, send, got, [part])
    (send,) = fold(place * 0, keep, send, swap(send, 4), [])
    outgoing.append(to_owners(tie(part, [send])))
    curvature = None
    if rows == 1:
        (curvature,) = unpack(outgoing[0], 0, chunk, 0, probe_count, None, [])
    send = pair(core, send, swap_probe(send, 1), block_rows, [])
    grad_qkv_weight, *small = join(
        upper, send, swap_probe(send, 2), block_rows, 3 * head_width, blocks, feature_width, [layer_out]
    )

    share_width = share.shape[2]
    half_width = part_width // 2
    if rows == 1:
        curvature, up_half, scores = unpack(outgoing[1], 1, chunk, share_width, probe_count, curvature, small[6:])
        grad_up_weight = spread(core, up_half, swap_probe(up_half, 1), blocks, half_width)
        scores = scores[0]
    else:
        whole_units = jnp.concatenate([got[:, :, : chunk * part_width] for got in outgoing], axis=2)
        whole_units = whole_units.reshape(blocks, local_rows, probe_count, rows, fine)
        curvature = whole_units.transpose(2, 1, 3, 0, 4).reshape(probe_count, local_rows, hidden_width)
        curvature = curvature.astype(F32)
        up_half = outgoing[1][:, :, chunk * part_width : chunk * part_width + half_width]
        both = lax.all_gather(up_half, "probe", axis_index_groups=[[0, 1], [2, 3]])
        both = both.transpose(2, 1, 0, 3).reshape(local_rows, blocks, rows, fine)
        grad_up_weight = both.transpose(0, 2, 1, 3).reshape(local_rows, hidden_width).astype(F32)
        scores = lax.psum(share[0, 0, -LANES:].astype(F32), "ex", axis_index_groups=row_groups)
    start = half_width % LANES
    scores = scores[start : start + probe_count] + scores[start + probe_count : start + 2 * probe_count]
    scores = scores[:, None]

    def over_groups(value):
        value = lax.all_gather(value, "ex", axis_index_groups=row_groups, tiled=True)
        return lax.dynamic_slice_in_dim(over_rows(value), place * local_rows, local_rows, 0)

    if rows > 1:
        grad_down = over_rows(grad_down)
        grad_qkv_weight, grad_out_weight = over_groups(grad_qkv_weight), over_groups(grad_out_weight)
        small = lax.psum(small, "ex", axis_index_groups=across)
        scores = lax.all_gather(scores, "ex", axis_index_groups=across, axis=1, tiled=True)
    sums, grad_qkv_bias, grad_up_bias = small[:5], small[5], small[6]
    if rows > 1:
        grad_up_bias = grad_up_bias.reshape(blocks, rows, fine).transpose(1, 0, 2).reshape(-1)
    return (
        layer_out,
        input_grad,
        grad_qkv_weight,
        grad_qkv_bias,
        grad_out_weight,
        sums[0],
        grad_up_weight,
        grad_up_bias,
        grad_down,
        sums[0],
        sums[3],
        sums[4],
        sums[1],
        sums[2],
        curvature,
        scores,
    )


def solution(mesh):
    in_specs = (
        P("ex", None),
        P(),
        P(),
        P(),
        P(),
        P(),
        P(),
        P(),
        P(),
        P(),
        P(),
        P(),
        P(),
        P(),
        P("probe", "ex", None),
        P("ex", None),
    )
    out_specs = (
        P("ex", None),
        P("ex", None),
        P("ex", None),
        P(),
        P("ex", None),
        P(),
        P("ex", None),
        P(),
        P("ex", None),
        P(),
        P(),
        P(),
        P(),
        P(),
        P("probe", "ex", None),
        P("probe", None),
    )
    return jax.shard_map(
        on_device, mesh=mesh, in_specs=in_specs, out_specs=out_specs, check_vma=False
    )
```

time: 1970 us -> 249 us (0.13)
  waiting for transfers between devices: 1460 us -> 63 us
  matrix products: 157 us -> 0 us
  blocking collectives: 154 us -> 0 us
  Pallas kernels: 0 us -> 106 us
  other arithmetic: 80.9 us -> 6.24 us
  local copies, waits for them, and re-layouts: 65.4 us -> 31.1 us
    reduce_scatter x5 -> x0, waiting for transfers between devices: 728 us -> none  [the longest x1 195 us: on_device(): lax.psum_scatter(jnp.einsum('tc,tq->cq', columns, weighted, preferred_ele...]
    all_gather x1 -> x0, waiting for transfers between devices: 345 us -> none  [on_device(): lax.all_gather(probe_dirs, 'ex', axis=1, tiled=True)]
    ppermute x14 -> x19, waiting for transfers between devices: 383 us -> 60.8 us  [the longest x9 35.4 us: swap(): return lax.ppermute(value, 'ex', [(i, i ^ distance) for i in range(groups)])]
    dot_general x62 -> x0, matrix products: 157 us -> none  [the longest x8 31.5 us: block_probs(): jnp.einsum('qhd,khd->hqk', attended_grad, kv_pack[1].reshape(head_shape),...]
    psum x1 -> x0, blocking collectives: 154 us -> none  [on_device(): probe_scores, small_total = lax.psum((score_term, small_flat), 'ex')]
    pallas_call x0 -> x23, Pallas kernels: none -> 106 us  [the longest x21 88.3 us: call(): pl.pallas_call(body, in_specs=list(in_specs) + [ANY] * spare, input_outpu...]
    convert_element_type x10 -> x2, other arithmetic: 39.6 us -> 1.33 us  [the longest x1 0.76 us: attention(): bias.astype(F32)[None]]
  transfers between devices with their start and end apart: 20 -> 22, of which waited for: 16 -> 14; matrix products, arithmetic and copies ran while one was open for 12% -> 5% of each run, Pallas kernels for 0% -> 39%
where the time goes in v1:
time: 249 us; the launch traced here: 247 us
  Pallas kernels  106 us (43%)
  waiting for transfers between devices  63 us (25%)
  starting transfers between devices  40.1 us (16%)
  local copies, waits for them, and re-layouts  31.1 us (12%)
  other arithmetic  6.24 us (3%)
    pallas_call x21, Pallas kernels, call(): pl.pallas_call(body, in_specs=list(in_specs) + [ANY] * spare, input_outpu...  88.3 us
    ppermute x9, waiting for transfers between devices, swap(): return lax.ppermute(value, 'ex', [(i, i ^ distance) for i in range(groups)])  35.4 us
    ppermute x10, waiting for transfers between devices, swap_probe(): lax.ppermute(value, 'probe', [(i, i ^ distance) for i in range(probe_grou...  25.4 us
    unnamed x110, local copies, waits for them, and re-layouts  24.6 us
    pallas_call x2, Pallas kernels, hidden_units(): pl.pallas_call(functools.partial(hidden_kernel, before is None), grid_spe...  17.7 us
    ppermute x9, starting transfers between devices, swap(): return lax.ppermute(value, 'ex', [(i, i ^ distance) for i in range(groups)])  14.5 us
    all_to_all x2, starting transfers between devices, to_owners(): lax.all_to_all(part, 'ex', 0, 0, axis_index_groups=row_groups, tiled=True)  11.2 us
    ppermute x10, starting transfers between devices, swap_probe(): lax.ppermute(value, 'probe', [(i, i ^ distance) for i in range(probe_grou...  9.88 us
  transfers between devices with their start and end apart: 22, of which 14 were waited for; matrix products, arithmetic and copies ran while one was open for 5% of the time, Pallas kernels for 39%

profile of v1, /device:TPU:1, one launch (start us, length us, event | category | flops | bytes accessed | tf_op | source)
XLA Modules:
  0.0 247.4 jit_solution(9413120198135974929)
XLA Ops:
  0.7 1.9 fusion.1.refs_0_
  2.7 2.0 collective-permute-start
  4.7 1.3 collective-permute-start.1
  6.0 1.6 fusion.3
  7.6 2.4 collective-permute-start.3
  13.2 11.0 %local.1 = (f32[256,768]{1,0:T(8,128)}, f32[256,768]{1,0:T(8,128)}, f32[8,768]{1,0:T(8,128)}) custom-call(bf16[256,768]{1,0:T(8,128)(2,1)} %refs_3_.5, bf16[256,768]{1,0:T(8,128)(2,1)} %refs_1_.3, bf16[768,3072]{1,0:T(8,128)(2,1)} %refs_9_.1, bf16[3072]{0:T(1024)(128)(2,1)} %refs_3_.4, bf16[3072,768]{1,0:T(8,128)(2,1)} %refs_11_.1, f32[8,768]{1,0:T(8,128)} %copy-done.30), custom_call_target="tpu_custom_call" | custom-call | flops 1000 | bytes 1000 | tf_op jit(solution)/shard_map/local/pallas_call | solution.py:98
  24.2 2.2 collective-permute-done.3.refs_4_
  26.4 7.1 %collective-permute-done.4.refs_5_ = bf16[1,2,64,768]{3,2,1,0:T(8,128)(2,1)} collective-permute-done((bf16[1,2,64,768]{3,2,1,0:T(8,128)(2,1)}, bf16[1,2,64,768]{3,2,1,0:T(8,128)(2,1)}, u32[]{:S(2)}, u32[]{:S(2)}) %collective-permute-start.4) | collective-permute-done | bytes 196640 | tf_op jit(solution)/shard_map/ppermute | solution.py:1011
  34.3 1.5 stack.36
  38.4 8.0 %collective-permute-done.8.refs_2_.refs_5_.refs_8_.refs_1_ = bf16[2,2,64,768]{3,2,1,0:T(8,128)(2,1)S(1)} collective-permute-done((bf16[2,2,64,768]{3,2,1,0:T(8,128)(2,1)S(1)}, bf16[2,2,64,768]{3,2,1,0:T(8,128)(2,1)S(1)}, u32[]{:S(2)}, u32[]{:S(2)}) %collective-permute-start.8) | collective-permute-done | bytes 393248 | tf_op jit(solution)/shard_map/ppermute | solution.py:1011
  47.1 1.4 copy-done.7
  49.3 4.5 %all-to-all-start = ((bf16[8,96,1536]{2,1,0:T(8,128)(2,1)}), bf16[8,96,1536]{2,1,0:T(8,128)(2,1)}, u32[]{:S(2)}, u32[]{:S(2)}) async-start(bf16[8,96,1536]{2,1,0:T(8,128)(2,1)} %copy-done.7), calls=%async_computation | async-start | bytes 4718592 | tf_op jit(solution)/shard_map/all_to_all | solution.py:1054
  53.8 2.9 %collective-permute-start.5 = (bf16[2,2,128,768]{3,2,1,0:T(8,128)(2,1)}, bf16[2,2,128,768]{3,2,1,0:T(8,128)(2,1)}, u32[]{:S(2)}, u32[]{:S(2)}) collective-permute-start(bf16[2,2,128,768]{3,2,1,0:T(8,128)(2,1)} %copy-done.21), channel_id=1, source_target_pairs={{0,8},{8,0},{16,24},{24,16},{1,9},{9,1},{17,25},{25,17},{2,10},{10... | collective-permute-start | bytes 2359304 | tf_op jit(solution)/shard_map/ppermute | solution.py:1014
  56.7 1.2 collective-permute-start.7
  60.0 8.3 %hidden_units.2 = (bf16[1024,768]{1,0:T(8,128)(2,1)}, bf16[768,1024]{1,0:T(8,128)(2,1)}, f32[1024,384]{1,0:T(8,128)}, f32[384,768]{1,0:T(8,128)}, f32[768,384]{1,0:T(8,128)}, /*index=5*/f32[1,384]{1,0:T(1,128)}) custom-call(s32[1]{0:T(128)} %bitcast.6.refs_0_, bf16[2,2,128,768]{3,2,1,0:T(8,128)(2,1)} %copy-done.21, ...), custom_call_target="tpu_custom_call" | custom-call | flops 1000 | bytes 1000 | tf_op jit(solution)/shard_map/hidden_units/pallas_call | solution.py:724
  68.4 7.4 %collective-permute-done.9.refs_3_.refs_6_.refs_9_ = bf16[2,2,64,768]{3,2,1,0:T(8,128)(2,1)} collective-permute-done((bf16[2,2,64,768]{3,2,1,0:T(8,128)(2,1)}, bf16[2,2,64,768]{3,2,1,0:T(8,128)(2,1)}, u32[]{:S(2)}, u32[]{:S(2)}) %collective-permute-start.9) | collective-permute-done | bytes 393248 | tf_op jit(solution)/shard_map/ppermute | solution.py:1014
  76.4 2.4 stack.37
  78.8 1.3 collective-permute-start.10
  80.1 1.4 copy.37.refs_20_
  83.3 1.4 constant_dynamic-slice_fusion.1.refs_14_
  84.7 2.5 %fusion.6 = (bf16[2,2,64,768]{3,2,1,0:T(8,128)(2,1)}, bf16[2,2,64,768]{3,2,1,0:T(8,128)(2,1)}, bf16[2,2,64,768]{3,2,1,0:T(8,128)(2,1)}, bf16[2,2,64,768]{3,2,1,0:T(8,128)(2,1)}) fusion(bf16[8,2,64,768]{3,2,1,0:T(8,128)(2,1)} %collective-permute-done.10), kind=kLoop, calls=%fused_computation.15 | loop fusion | bytes 3145728 | tf_op jit(solution)/shard_map/slice | solution.py:1062
  87.3 9.3 %hidden_units.3 = (bf16[1024,768]{1,0:T(8,128)(2,1)}, bf16[768,1024]{1,0:T(8,128)(2,1)}, f32[1024,384]{1,0:T(8,128)}, f32[384,768]{1,0:T(8,128)}, f32[768,384]{1,0:T(8,128)}, /*index=5*/f32[1,384]{1,0:T(1,128)}) custom-call(s32[1]{0:T(128)} %bitcast.6.refs_0_, bf16[2,2,64,768]{3,2,1,0:T(8,128)(2,1)} %copy-done.14, ...), custom_call_target="tpu_custom_call" | custom-call | flops 1000 | bytes 1000 | tf_op jit(solution)/shard_map/hidden_units/pallas_call | solution.py:724
  97.5 33.0 %attention.1 = (bf16[352,960]{1,0:T(8,128)(2,1)}, bf16[4,96,640]{2,1,0:T(8,128)(2,1)}, bf16[448,640]{1,0:T(8,128)(2,1)}) custom-call(bf16[2,2,128,768]{3,2,1,0:T(8,128)(2,1)} %copy-done.21, bf16[2,2,128,768]{3,2,1,0:T(8,128)(2,1)} %collective-permute-done.5.refs_2_.refs_1_, bf16[2,2,128,768]{3,2,1,0:T(8,128)(2,1)} %copy-done.22, ...), custom_call_target="tpu_custom_call" | custom-call | flops 1000 | bytes 1000 | tf_op jit(solution)/shard_map/attention/pallas_call | solution.py:98
  130.5 1.5 collective-permute-start.13
  134.3 10.3 %curvature.2.refs_4_.refs_0_ = bf16[8,96,768]{2,1,0:T(8,128)(2,1)} custom-call(bf16[768,1536]{1,0:T(8,128)(2,1)} %bitcast.13.refs_1_.refs_0_, bf16[1024,768]{1,0:T(8,128)(2,1)} %get-tuple-element.66.refs_1_, bf16[768,1024]{1,0:T(8,128)(2,1)} %get-tuple-element.67.refs_2_, f32[1024,384]{1,0:T(8,128)} %get-tuple-element.68.refs_3_, ...), custom_call_target="tpu_custom_call" | custom-call | flops 1000 | bytes 1000 | tf_op jit(solution)/shard_map/curvature/pallas_call | solution.py:98
  144.8 1.3 copy-done.4
  146.1 2.0 fold.3
  148.8 5.5 %all-to-all-start.2 = ((bf16[8,96,768]{2,1,0:T(8,128)(2,1)}), bf16[8,96,768]{2,1,0:T(8,128)(2,1)}, u32[]{:S(2)}, u32[]{:S(2)}) async-start(bf16[8,96,768]{2,1,0:T(8,128)(2,1)} %tie.3), calls=%async_computation.2 | async-start | bytes 2359296 | tf_op jit(solution)/shard_map/all_to_all | solution.py:1090
  154.3 1.5 collective-permute-start.14
  155.7 2.4 share.1.refs_7_
  158.9 10.1 %curvature.3.refs_8_.refs_4_ = bf16[8,96,1024]{2,1,0:T(8,128)(2,1)} custom-call(bf16[768,1536]{1,0:T(8,128)(2,1)} %bitcast.13.refs_1_.refs_0_, bf16[1024,768]{1,0:T(8,128)(2,1)} %get-tuple-element.66.refs_1_, bf16[768,1024]{1,0:T(8,128)(2,1)} %get-tuple-element.67.refs_2_, f32[1024,384]{1,0:T(8,128)} %get-tuple-element.68.refs_3_, ...), custom_call_target="tpu_custom_call" | custom-call | flops 1000 | bytes 1000 | tf_op jit(solution)/shard_map/curvature/pallas_call | solution.py:98
  169.0 10.2 %collective-permute-done.14.refs_3_ = bf16[256,640]{1,0:T(8,128)(2,1)} collective-permute-done((bf16[256,640]{1,0:T(8,128)(2,1)}, bf16[256,640]{1,0:T(8,128)(2,1)}, u32[]{:S(2)}, u32[]{:S(2)}) %collective-permute-start.14) | collective-permute-done | bytes 327712 | tf_op jit(solution)/shard_map/ppermute | solution.py:1011
  179.2 1.4 copy-done.2
  180.6 1.3 fold.4
  181.9 4.4 %collective-permute-start.15 = (bf16[160,640]{1,0:T(8,128)(2,1)S(1)}, bf16[160,640]{1,0:T(8,128)(2,1)S(1)}, u32[]{:S(2)}, u32[]{:S(2)}) collective-permute-start(bf16[160,640]{1,0:T(8,128)(2,1)S(1)} %get-tuple-element.80.refs_2_), channel_id=1, source_target_pairs={{0,4},{1,5},{2,6},{3,7},{4,0},{5,1},{6,2},{7,3},{8,12},{9,13},{10,... | collective-permute-start | bytes 614408 | tf_op jit(solution)/shard_map/ppermute | solution.py:1011
  187.5 7.7 %collective-permute-done.15.refs_3_ = bf16[160,640]{1,0:T(8,128)(2,1)S(1)} collective-permute-done((bf16[160,640]{1,0:T(8,128)(2,1)S(1)}, bf16[160,640]{1,0:T(8,128)(2,1)S(1)}, u32[]{:S(2)}, u32[]{:S(2)}) %collective-permute-start.15) | collective-permute-done | bytes 204832 | tf_op jit(solution)/shard_map/ppermute | solution.py:1011
  196.0 5.7 %all-to-all-start.1 = ((bf16[8,96,1024]{2,1,0:T(8,128)(2,1)}), bf16[8,96,1024]{2,1,0:T(8,128)(2,1)}, u32[]{:S(2)}, u32[]{:S(2)}) async-start(bf16[8,96,1024]{2,1,0:T(8,128)(2,1)} %tie.2), calls=%async_computation.1 | async-start | bytes 3145728 | tf_op jit(solution)/shard_map/all_to_all | solution.py:1090
  201.7 1.3 collective-permute-start.12
  206.2 14.5 %collective-permute-done.12.refs_2_ = bf16[352,1152]{1,0:T(8,128)(2,1)} collective-permute-done((bf16[352,1152]{1,0:T(8,128)(2,1)S(1)}, bf16[352,1152]{1,0:T(8,128)(2,1)}, u32[]{:S(2)}, u32[]{:S(2)}) %collective-permute-start.12) | collective-permute-done | bytes 811040 | tf_op jit(solution)/shard_map/ppermute | solution.py:1014
  222.9 1.3 copy-done.27
  227.2 2.8 %finish.1 = (bf16[256,768]{1,0:T(8,128)(2,1)}, bf16[256,768]{1,0:T(8,128)(2,1)}, f32[96,768]{1,0:T(8,128)}) custom-call(s32[1]{0:T(128)} %bitcast.refs_0_, bf16[352,1152]{1,0:T(8,128)(2,1)S(1)} %copy-done.10, bf16[352,1152]{1,0:T(8,128)(2,1)} %collective-permute-done.12.refs_2_, bf16[256,768]{1,0:T(8,128)(2,1)S(1)} %copy-done.6, f32[256,768]{1,0:T(8,128)S(1)} %copy-done.33, ...), custom_call_target="tpu_custom_call" | custom-call | flops 1000 | bytes 1000 | tf_op jit(solution)/shard_map/finish/pallas_call | solution.py:98
  231.0 2.2 join.1
  233.2 2.8 %unpack.2.refs_1_ = f32[4,96,3072]{2,1,0:T(8,128)} custom-call(bf16[8,96,768]{2,1,0:T(8,128)(2,1)} %all-to-all-done.2.refs_0_), custom_call_target="tpu_custom_call" | custom-call | flops 1000 | bytes 1000 | tf_op jit(solution)/shard_map/unpack/pallas_call | solution.py:98
  236.0 2.2 all-to-all-done.1.refs_0_
  238.2 3.3 %unpack.3 = (f32[4,96,3072]{2,1,0:T(8,128)}, bf16[96,2048]{1,0:T(8,128)(2,1)}, f32[16,128]{1,0:T(8,128)}) custom-call(bf16[8,96,1024]{2,1,0:T(8,128)(2,1)} %all-to-all-done.1.refs_0_, f32[4,96,3072]{2,1,0:T(8,128)} %unpack.2.refs_1_, f32[3072]{0:T(1024)} %get-tuple-element.121.refs_2_), custom_call_target="tpu_custom_call", output_to_operand_aliasing={{0}: (1, {})} | custom-call | flops 1000 | bytes 1000 | tf_op jit(solution)/shard_map/unpack/pallas_call | solution.py:98
  241.4 1.6 collective-permute-start.18
  243.1 1.3 add_bitcast_fusion
  245.6 1.2 spread.1
  (141 shorter events, 30.2 us)
Async XLA Ops:
  0.6 82.7 %copy-start = (bf16[768,2304]{1,0:T(8,128)(2,1)S(1)}, bf16[768,2304]{1,0:T(8,128)(2,1)}, u32[]{:S(2)}) copy-start(bf16[768,2304]{1,0:T(8,128)(2,1)} %param.20) | copy-start | bytes 10616836
  0.7 10.5 %copy-start.44 = (f32[768]{0:T(1024)S(1)}, f32[768]{0:T(1024)}, u32[]{:S(2)}) copy-start(f32[768]{0:T(1024)} %refs_0_.3) | copy-start | bytes 9220
  0.7 10.5 %copy-start.45 = (f32[768]{0:T(1024)S(1)}, f32[768]{0:T(1024)}, u32[]{:S(2)}) copy-start(f32[768]{0:T(1024)} %refs_1_.2) | copy-start | bytes 9220
  0.7 10.5 %copy-start.46 = (f32[768]{0:T(1024)S(1)}, f32[768]{0:T(1024)}, u32[]{:S(2)}) copy-start(f32[768]{0:T(1024)} %refs_2_.2) | copy-start | bytes 9220
  0.7 10.5 %copy-start.47 = (f32[768]{0:T(1024)S(1)}, f32[768]{0:T(1024)}, u32[]{:S(2)}) copy-start(f32[768]{0:T(1024)} %refs_3_.3) | copy-start | bytes 9220
  2.7 30.9 %collective-permute-start = (bf16[1,2,128,768]{3,2,1,0:T(8,128)(2,1)}, bf16[1,2,128,768]{3,2,1,0:T(8,128)(2,1)}, u32[]{:S(2)}, u32[]{:S(2)}) collective-permute-start(bf16[1,2,128,768]{3,2,1,0:T(8,128)(2,1)} %fusion.1.refs_0_), channel_id=1, source_target_pairs={{0,1},{1,0},{2,3},{3,2},{4,5},{5,4},{6,7},{7,6},{8,9},{9,8},{10,11... | collective-permute-start | bytes 1179656 | tf_op jit(solution)/shard_map/ppermute | solution.py:1011
  4.7 28.9 %collective-permute-start.1 = (bf16[1,2,128,768]{3,2,1,0:T(8,128)(2,1)}, bf16[1,2,128,768]{3,2,1,0:T(8,128)(2,1)}, u32[]{:S(2)}, u32[]{:S(2)}) collective-permute-start(bf16[1,2,128,768]{3,2,1,0:T(8,128)(2,1)} %fusion.1.refs_0_), channel_id=1, source_target_pairs={{0,2},{1,3},{2,0},{3,1},{4,6},{5,7},{6,4},{7,5},{8,10},{9,11},{10,... | collective-permute-start | bytes 1179656 | tf_op jit(solution)/shard_map/ppermute | solution.py:1011
  6.0 27.6 %collective-permute-start.2 = (bf16[1,2,128,768]{3,2,1,0:T(8,128)(2,1)}, bf16[1,2,128,768]{3,2,1,0:T(8,128)(2,1)}, u32[]{:S(2)}, u32[]{:S(2)}) collective-permute-start(bf16[1,2,128,768]{3,2,1,0:T(8,128)(2,1)} %fusion.1.refs_0_), channel_id=1, source_target_pairs={{0,3},{1,2},{2,1},{3,0},{4,7},{5,6},{6,5},{7,4},{8,11},{9,10},{10,... | collective-permute-start | bytes 1179656 | tf_op jit(solution)/shard_map/ppermute | solution.py:1011
  7.6 18.8 %collective-permute-start.3 = (bf16[1,2,64,768]{3,2,1,0:T(8,128)(2,1)}, bf16[1,2,64,768]{3,2,1,0:T(8,128)(2,1)S(1)}, u32[]{:S(2)}, u32[]{:S(2)}) collective-permute-start(bf16[1,2,64,768]{3,2,1,0:T(8,128)(2,1)} %fusion.3), channel_id=1, source_target_pairs={{0,4},{1,5},{2,6},{3,7},{4,0},{5,1},{6,2},{7,3},{8,12},{9,13},{10,... | collective-permute-start | bytes 589832 | tf_op jit(solution)/shard_map/ppermute | solution.py:1011
  10.1 23.5 %collective-permute-start.4 = (bf16[1,2,64,768]{3,2,1,0:T(8,128)(2,1)}, bf16[1,2,64,768]{3,2,1,0:T(8,128)(2,1)}, u32[]{:S(2)}, u32[]{:S(2)}) collective-permute-start(bf16[1,2,64,768]{3,2,1,0:T(8,128)(2,1)} %fusion.3), channel_id=1, source_target_pairs={{0,6},{1,7},{2,4},{3,5},{4,2},{5,3},{6,0},{7,1},{8,14},{9,15},{10,... | collective-permute-start | bytes 589832 | tf_op jit(solution)/shard_map/ppermute | solution.py:1011
  13.2 33.2 %copy-start.24 = (bf16[4,96,3072]{2,1,0:T(8,128)(2,1)S(1)}, bf16[4,96,3072]{2,1,0:T(8,128)(2,1)}, u32[]{:S(2)}) copy-start(bf16[4,96,3072]{2,1,0:T(8,128)(2,1)} %refs_0_.5) | copy-start | bytes 7077892
  37.6 8.7 %collective-permute-start.8 = (bf16[2,2,64,768]{3,2,1,0:T(8,128)(2,1)S(1)}, bf16[2,2,64,768]{3,2,1,0:T(8,128)(2,1)S(1)}, u32[]{:S(2)}, u32[]{:S(2)}) collective-permute-start(bf16[2,2,64,768]{3,2,1,0:T(8,128)(2,1)S(1)} %get-tuple-element.58.refs_0_.refs_1_.refs_4_), channel_id=1, source_target_pairs={{0,1},{1,0},{2,3},{3,2},{4,5},{5,4},{6,7},{7,6},{8,9},{9,8},{10,11... | collective-permute-start | bytes 1179656 | tf_op jit(solution)/shard_map/ppermute | solution.py:1011
  49.3 8.9 %copy-start.51 = (bf16[3072]{0:T(1024)(128)(2,1)S(1)}, bf16[3072]{0:T(1024)(128)(2,1)}, u32[]{:S(2)}) copy-start(bf16[3072]{0:T(1024)(128)(2,1)} %refs_3_.4) | copy-start | bytes 18436
  49.3 85.0 %all-to-all-start = ((bf16[8,96,1536]{2,1,0:T(8,128)(2,1)}), bf16[8,96,1536]{2,1,0:T(8,128)(2,1)}, u32[]{:S(2)}, u32[]{:S(2)}) async-start(bf16[8,96,1536]{2,1,0:T(8,128)(2,1)} %copy-done.7), calls=%async_computation | async-start | bytes 4718592 | tf_op jit(solution)/shard_map/all_to_all | solution.py:1054
  53.8 5.1 %collective-permute-start.5 = (bf16[2,2,128,768]{3,2,1,0:T(8,128)(2,1)}, bf16[2,2,128,768]{3,2,1,0:T(8,128)(2,1)}, u32[]{:S(2)}, u32[]{:S(2)}) collective-permute-start(bf16[2,2,128,768]{3,2,1,0:T(8,128)(2,1)} %copy-done.21), channel_id=1, source_target_pairs={{0,8},{8,0},{16,24},{24,16},{1,9},{9,1},{17,25},{25,17},{2,10},{10... | collective-permute-start | bytes 2359304 | tf_op jit(solution)/shard_map/ppermute | solution.py:1014
  56.7 3.4 %collective-permute-start.6 = (bf16[2,2,128,768]{3,2,1,0:T(8,128)(2,1)}, bf16[2,2,128,768]{3,2,1,0:T(8,128)(2,1)}, u32[]{:S(2)}, u32[]{:S(2)}) collective-permute-start(bf16[2,2,128,768]{3,2,1,0:T(8,128)(2,1)} %copy-done.22), channel_id=1, source_target_pairs={{0,8},{8,0},{16,24},{24,16},{1,9},{9,1},{17,25},{25,17},{2,10},{10... | collective-permute-start | bytes 2359304 | tf_op jit(solution)/shard_map/ppermute | solution.py:1014
  56.7 11.6 %collective-permute-start.7 = (bf16[2,2,64,768]{3,2,1,0:T(8,128)(2,1)}, bf16[2,2,64,768]{3,2,1,0:T(8,128)(2,1)}, u32[]{:S(2)}, u32[]{:S(2)}) collective-permute-start(bf16[2,2,64,768]{3,2,1,0:T(8,128)(2,1)} %copy-done.14), channel_id=1, source_target_pairs={{0,16},{8,24},{16,0},{24,8},{1,17},{9,25},{17,1},{25,9},{2,18},{10... | collective-permute-start | bytes 1179656 | tf_op jit(solution)/shard_map/ppermute | solution.py:1014
  58.0 17.8 %collective-permute-start.9 = (bf16[2,2,64,768]{3,2,1,0:T(8,128)(2,1)}, bf16[2,2,64,768]{3,2,1,0:T(8,128)(2,1)}, u32[]{:S(2)}, u32[]{:S(2)}) collective-permute-start(bf16[2,2,64,768]{3,2,1,0:T(8,128)(2,1)} %copy-done.11), channel_id=1, source_target_pairs={{0,16},{8,24},{16,0},{24,8},{1,17},{9,25},{17,1},{25,9},{2,18},{10... | collective-permute-start | bytes 1179656 | tf_op jit(solution)/shard_map/ppermute | solution.py:1014
  60.0 15.7 %copy-start.12 = (bf16[2,2,64,768]{3,2,1,0:T(8,128)(2,1)S(1)}, bf16[2,2,64,768]{3,2,1,0:T(8,128)(2,1)}, u32[]{:S(2)}) copy-start(bf16[2,2,64,768]{3,2,1,0:T(8,128)(2,1)} %copy-done.11) | copy-start | bytes 1179652
  60.0 15.7 %copy-start.15 = (bf16[2,2,64,768]{3,2,1,0:T(8,128)(2,1)S(1)}, bf16[2,2,64,768]{3,2,1,0:T(8,128)(2,1)}, u32[]{:S(2)}) copy-start(bf16[2,2,64,768]{3,2,1,0:T(8,128)(2,1)} %copy-done.14) | copy-start | bytes 1179652
  78.8 5.9 %collective-permute-start.10 = (bf16[8,2,64,768]{3,2,1,0:T(8,128)(2,1)}, bf16[8,2,64,768]{3,2,1,0:T(8,128)(2,1)}, u32[]{:S(2)}, u32[]{:S(2)}) collective-permute-start(bf16[8,2,64,768]{3,2,1,0:T(8,128)(2,1)} %stack.37), channel_id=1, source_target_pairs={{0,8},{8,0},{16,24},{24,16},{1,9},{9,1},{17,25},{25,17},{2,10},{10... | collective-permute-start | bytes 4718600 | tf_op jit(solution)/shard_map/ppermute | solution.py:1014
  87.3 9.4 %copy-start.5 = (bf16[256,768]{1,0:T(8,128)(2,1)S(1)}, bf16[256,768]{1,0:T(8,128)(2,1)}, u32[]{:S(2)}) copy-start(bf16[256,768]{1,0:T(8,128)(2,1)} %refs_3_.5) | copy-start | bytes 1179652
  87.3 9.4 %copy-start.13 = (bf16[2,2,64,768]{3,2,1,0:T(8,128)(2,1)S(1)}, bf16[2,2,64,768]{3,2,1,0:T(8,128)(2,1)}, u32[]{:S(2)}) copy-start(bf16[2,2,64,768]{3,2,1,0:T(8,128)(2,1)} %copy-done.11) | copy-start | bytes 1179652
  87.3 9.4 %copy-start.16 = (bf16[2,2,64,768]{3,2,1,0:T(8,128)(2,1)S(1)}, bf16[2,2,64,768]{3,2,1,0:T(8,128)(2,1)}, u32[]{:S(2)}) copy-start(bf16[2,2,64,768]{3,2,1,0:T(8,128)(2,1)} %copy-done.14) | copy-start | bytes 1179652
  87.3 9.4 %copy-start.17 = (bf16[2,2,64,768]{3,2,1,0:T(8,128)(2,1)S(1)}, bf16[2,2,64,768]{3,2,1,0:T(8,128)(2,1)}, u32[]{:S(2)}) copy-start(bf16[2,2,64,768]{3,2,1,0:T(8,128)(2,1)} %get-tuple-element.94.refs_8_.refs_11_) | copy-start | bytes 1179652
  87.3 9.4 %copy-start.18 = (bf16[2,2,64,768]{3,2,1,0:T(8,128)(2,1)S(1)}, bf16[2,2,64,768]{3,2,1,0:T(8,128)(2,1)}, u32[]{:S(2)}) copy-start(bf16[2,2,64,768]{3,2,1,0:T(8,128)(2,1)} %get-tuple-element.95.refs_7_.refs_10_) | copy-start | bytes 1179652
  87.3 9.4 %copy-start.19 = (bf16[2,2,64,768]{3,2,1,0:T(8,128)(2,1)S(1)}, bf16[2,2,64,768]{3,2,1,0:T(8,128)(2,1)}, u32[]{:S(2)}) copy-start(bf16[2,2,64,768]{3,2,1,0:T(8,128)(2,1)} %get-tuple-element.96.refs_4_.refs_7_) | copy-start | bytes 1179652
  87.3 9.4 %copy-start.20 = (bf16[2,2,64,768]{3,2,1,0:T(8,128)(2,1)S(1)}, bf16[2,2,64,768]{3,2,1,0:T(8,128)(2,1)}, u32[]{:S(2)}) copy-start(bf16[2,2,64,768]{3,2,1,0:T(8,128)(2,1)} %get-tuple-element.97.refs_3_.refs_6_) | copy-start | bytes 1179652
  87.3 9.4 %copy-start.31 = (f32[8,768]{1,0:T(8,128)S(1)}, f32[8,768]{1,0:T(8,128)}, u32[]{:S(2)}) copy-start(f32[8,768]{1,0:T(8,128)} %copy-done.30) | copy-start | bytes 73732
  87.3 9.4 %copy-start.42 = (f32[8,768]{1,0:T(8,128)S(1)}, f32[8,768]{1,0:T(8,128)}, u32[]{:S(2)}) copy-start(f32[8,768]{1,0:T(8,128)} %get-tuple-element.55.refs_6_.refs_21_) | copy-start | bytes 73732
  130.4 2.4 collective-permute-start.11
  130.5 14.3 %collective-permute-start.13 = (bf16[448,640]{1,0:T(8,128)(2,1)}, bf16[448,640]{1,0:T(8,128)(2,1)}, u32[]{:S(2)}, u32[]{:S(2)}) collective-permute-start(bf16[448,640]{1,0:T(8,128)(2,1)} %get-tuple-element.74.refs_2_), channel_id=1, source_target_pairs={{0,1},{1,0},{2,3},{3,2},{4,5},{5,4},{6,7},{7,6},{8,9},{9,8},{10,11... | collective-permute-start | bytes 1720328 | tf_op jit(solution)/shard_map/ppermute | solution.py:1011
  134.3 10.4 %copy-start.8 = (bf16[352,1152]{1,0:T(8,128)(2,1)}, bf16[352,1152]{1,0:T(8,128)(2,1)S(1)}, u32[]{:S(2)}) copy-start(bf16[352,1152]{1,0:T(8,128)(2,1)S(1)} %merge.1.refs_1_.refs_2_) | copy-start | bytes 2433028
  134.3 10.5 %copy-start.35 = (bf16[448,640]{1,0:T(8,128)(2,1)S(1)}, bf16[448,640]{1,0:T(8,128)(2,1)}, u32[]{:S(2)}) copy-start(bf16[448,640]{1,0:T(8,128)(2,1)} %get-tuple-element.74.refs_2_) | copy-start | bytes 1720324
  134.3 10.5 %copy-start.36 = (bf16[4,96,640]{2,1,0:T(8,128)(2,1)S(1)}, bf16[4,96,640]{2,1,0:T(8,128)(2,1)}, u32[]{:S(2)}) copy-start(bf16[4,96,640]{2,1,0:T(8,128)(2,1)} %get-tuple-element.73.refs_1_) | copy-start | bytes 1474564
  148.8 7.0 %copy-start.29 = (f32[768,384]{1,0:T(8,128)S(1)}, f32[768,384]{1,0:T(8,128)}, u32[]{:S(2)}) copy-start(f32[768,384]{1,0:T(8,128)} %get-tuple-element.72.refs_2_) | copy-start | bytes 3538948
  148.8 47.2 %all-to-all-start.2 = ((bf16[8,96,768]{2,1,0:T(8,128)(2,1)}), bf16[8,96,768]{2,1,0:T(8,128)(2,1)}, u32[]{:S(2)}, u32[]{:S(2)}) async-start(bf16[8,96,768]{2,1,0:T(8,128)(2,1)} %tie.3), calls=%async_computation.2 | async-start | bytes 2359296 | tf_op jit(solution)/shard_map/all_to_all | solution.py:1090
  154.3 24.9 %collective-permute-start.14 = (bf16[256,640]{1,0:T(8,128)(2,1)}, bf16[256,640]{1,0:T(8,128)(2,1)}, u32[]{:S(2)}, u32[]{:S(2)}) collective-permute-start(bf16[256,640]{1,0:T(8,128)(2,1)} %get-tuple-element.75.refs_8_.refs_2_.refs_1_), channel_id=1, source_target_pairs={{0,2},{1,3},{2,0},{3,1},{4,6},{5,7},{6,4},{7,5},{8,10},{9,11},{10,... | collective-permute-start | bytes 983048 | tf_op jit(solution)/shard_map/ppermute | solution.py:1011
  158.9 20.3 %copy-start.40 = (bf16[2,96,640]{2,1,0:T(8,128)(2,1)S(1)}, bf16[2,96,640]{2,1,0:T(8,128)(2,1)}, u32[]{:S(2)}) copy-start(bf16[2,96,640]{2,1,0:T(8,128)(2,1)} %copy-done.39) | copy-start | bytes 737284
  180.6 5.8 %copy-start.3 = (bf16[8,96,1024]{2,1,0:T(8,128)(2,1)S(1)}, bf16[8,96,1024]{2,1,0:T(8,128)(2,1)}, u32[]{:S(2)}) copy-start(bf16[8,96,1024]{2,1,0:T(8,128)(2,1)} %curvature.3.refs_8_.refs_4_) | copy-start | bytes 4718596
  181.9 13.3 %collective-permute-start.15 = (bf16[160,640]{1,0:T(8,128)(2,1)S(1)}, bf16[160,640]{1,0:T(8,128)(2,1)S(1)}, u32[]{:S(2)}, u32[]{:S(2)}) collective-permute-start(bf16[160,640]{1,0:T(8,128)(2,1)S(1)} %get-tuple-element.80.refs_2_), channel_id=1, source_target_pairs={{0,4},{1,5},{2,6},{3,7},{4,0},{5,1},{6,2},{7,3},{8,12},{9,13},{10,... | collective-permute-start | bytes 614408 | tf_op jit(solution)/shard_map/ppermute | solution.py:1011
  196.0 7.1 %copy-start.26 = (bf16[160,640]{1,0:T(8,128)(2,1)S(1)}, bf16[160,640]{1,0:T(8,128)(2,1)}, u32[]{:S(2)}) copy-start(bf16[160,640]{1,0:T(8,128)(2,1)} %copy-done.25) | copy-start | bytes 614404
  196.0 42.2 %all-to-all-start.1 = ((bf16[8,96,1024]{2,1,0:T(8,128)(2,1)}), bf16[8,96,1024]{2,1,0:T(8,128)(2,1)}, u32[]{:S(2)}, u32[]{:S(2)}) async-start(bf16[8,96,1024]{2,1,0:T(8,128)(2,1)} %tie.2), calls=%async_computation.1 | async-start | bytes 3145728 | tf_op jit(solution)/shard_map/all_to_all | solution.py:1090
  201.7 19.0 %collective-permute-start.12 = (bf16[352,1152]{1,0:T(8,128)(2,1)S(1)}, bf16[352,1152]{1,0:T(8,128)(2,1)}, u32[]{:S(2)}, u32[]{:S(2)}) collective-permute-start(bf16[352,1152]{1,0:T(8,128)(2,1)S(1)} %copy-done.9), channel_id=1, source_target_pairs={{0,16},{8,24},{16,0},{24,8},{1,17},{9,25},{17,1},{25,9},{2,18},{10... | collective-permute-start | bytes 2433032 | tf_op jit(solution)/shard_map/ppermute | solution.py:1014
  203.1 2.1 collective-permute-start.16
  206.0 24.0 %collective-permute-start.17 = (bf16[160,1280]{1,0:T(8,128)(2,1)}, bf16[160,1280]{1,0:T(8,128)(2,1)}, u32[]{:S(2)}, u32[]{:S(2)}) collective-permute-start(bf16[160,1280]{1,0:T(8,128)(2,1)} %pair.1.refs_1_), channel_id=1, source_target_pairs={{0,16},{8,24},{16,0},{24,8},{1,17},{9,25},{17,1},{25,9},{2,18},{10... | collective-permute-start | bytes 1228808 | tf_op jit(solution)/shard_map/ppermute | solution.py:1014
  238.2 9.2 %copy-start.1 = (bf16[768,2304]{1,0:T(8,128)(2,1)S(1)}, bf16[768,2304]{1,0:T(8,128)(2,1)}, u32[]{:S(2)}) copy-start(bf16[768,2304]{1,0:T(8,128)(2,1)} %param.20) | copy-start | bytes 10616836
  241.4 3.2 %collective-permute-start.18 = (bf16[96,2048]{1,0:T(8,128)(2,1)}, bf16[96,2048]{1,0:T(8,128)(2,1)S(1)}, u32[]{:S(2)}, u32[]{:S(2)}) collective-permute-start(bf16[96,2048]{1,0:T(8,128)(2,1)} %get-tuple-element.86.refs_1_), channel_id=1, source_target_pairs={{0,8},{8,0},{16,24},{24,16},{1,9},{9,1},{17,25},{25,17},{2,10},{10... | collective-permute-start | bytes 1179656 | tf_op jit(solution)/shard_map/ppermute | solution.py:1014
  (28 other events, 37.9 us)
